TPU v7x, 128 devices: a whole 4x4x4 slice. The times are simulated.
128 devices in a mesh: rep: 16 (over x_hi, y, core), shard: 8 (over z, x_lo).
Axes of the slice: x: 4 (x_hi: 2, x_lo: 2; x = x_hi * 2 + x_lo), y: 4, z: 4, core: 2. Of those that a mesh axis runs over, the one named last changes fastest.
Arguments:
- hidden_in: bfloat16 [16384, 1024], P(('rep', 'shard')), may hold values from -6 to 6
- out_grad: bfloat16 [16384, 1024], P(('rep', 'shard')), may hold values from -6 to 6
- segment_ids: int32 [16384], P(('rep', 'shard')), may hold values from 0 to 1023, as said below
- first_gain: bfloat16 [1024], P('shard'), may hold values from 0.25 to 1.75
- first_shift: bfloat16 [1024], P('shard'), may hold values from -1.75 to 1.75
- second_gain: bfloat16 [1024], P('shard'), may hold values from 0.25 to 1.75
- second_shift: bfloat16 [1024], P('shard'), may hold values from -1.75 to 1.75
- qkv_weight: bfloat16 [1024, 3072], P('shard'), may hold values from -0.1875 to 0.1875
- qkv_bias: bfloat16 [3072], P('shard'), may hold values from -1.75 to 1.75
- dense_weight: bfloat16 [1024, 1024], P('shard'), may hold values from -2 to 2
- dense_bias: bfloat16 [1024], P('shard'), may hold values from -1.75 to 1.75
- up_weight: bfloat16 [1024, 4096], P('shard'), may hold values from -0.1875 to 0.1875
- up_bias: bfloat16 [4096], P('shard'), may hold values from -1.75 to 1.75
- down_weight: bfloat16 [4096, 1024], P('shard'), may hold values from -0.09375 to 0.09375
- down_bias: bfloat16 [1024], P('shard'), may hold values from -1.75 to 1.75
Outputs:
- output: bfloat16 [16384, 1024], P(('rep', 'shard'))
- input_grad: bfloat16 [16384, 1024], P(('rep', 'shard'))
- grad_first_gain: float32 [1024], P('shard')
- grad_first_shift: float32 [1024], P('shard')
- grad_second_gain: float32 [1024], P('shard')
- grad_second_shift: float32 [1024], P('shard')
- grad_qkv_weight: float32 [1024, 3072], P('shard')
- grad_qkv_bias: float32 [3072], P('shard')
- grad_dense_weight: float32 [1024, 1024], P('shard')
- grad_dense_bias: float32 [1024], P('shard')
- grad_up_weight: float32 [1024, 4096], P('shard')
- grad_up_bias: float32 [4096], P('shard')
- grad_down_weight: float32 [4096, 1024], P('shard')
- grad_down_bias: float32 [1024], P('shard')
Inputs may be any that keep to these rules, and one draw needn't show every extreme that they name: `segment_ids`: along each packed row of 1024 tokens the ids start at 0 and never fall; equal ids in a row are one document. The last document of every row has id 1024 - 1. In every row one document begins within the row's first 128 tokens and ends within its last 128 tokens.
All inputs are finite; a program needn't handle non-finite values.
Results may differ from a plain program's by a relative error of at most 0.011.
Values may be sent and summed in bfloat16 or wider, within the bound.
A program may use at most 192 MiB of HBM per device.

v0:
```python
from functools import partial

import jax
import jax.numpy as jnp
from jax import lax
from jax.sharding import PartitionSpec as P

HEADS = 16


def layer_norm(values, gain, shift):
    center = values - jnp.mean(values, axis=-1, keepdims=True)
    spread = jnp.mean(center * center, axis=-1, keepdims=True)
    return center * lax.rsqrt(spread + 1e-05) * gain + shift


def angle_tables(positions, rotary):
    inverse = jnp.power(10000.0, -jnp.arange(0, rotary, 2, dtype=jnp.float32) / rotary)
    angles = positions[:, None] * inverse[None, :]
    doubled = jnp.concatenate([angles, angles], axis=1)
    return (jnp.cos(doubled), jnp.sin(doubled))


def rotate(tensor, cosine, sine):
    rotary = cosine.shape[1]
    half = rotary // 2
    part = tensor[..., :rotary]
    turned = jnp.concatenate([-part[..., half:], part[..., :half]], axis=-1)
    moved = part * cosine[:, None, :] + turned * sine[:, None, :]
    return jnp.concatenate([moved, tensor[..., rotary:]], axis=-1)


def inner_rows(left, right):
    return lax.dot_general(
        left, right, (((0,), (0,)), ((), ())), preferred_element_type=jnp.float32
    )


def against(left, right):
    return lax.dot_general(
        left, right, (((1,), (1,)), ((), ())), preferred_element_type=jnp.float32
    )


def shards(
    hidden_in,
    out_grad,
    segment_ids,
    first_gain,
    first_shift,
    second_gain,
    second_shift,
    qkv_weight,
    qkv_bias,
    dense_weight,
    dense_bias,
    up_weight,
    up_bias,
    down_weight,
    down_bias,
):
    local_rows = hidden_in.shape[0]
    width = hidden_in.shape[1]
    size = width // HEADS
    own = lax.axis_index("shard")
    gathered = (
        lax.all_gather(first_gain, "shard", axis=0, tiled=True),
        lax.all_gather(first_shift, "shard", axis=0, tiled=True),
        lax.all_gather(second_gain, "shard", axis=0, tiled=True),
        lax.all_gather(second_shift, "shard", axis=0, tiled=True),
        lax.all_gather(qkv_weight, "shard", axis=0, tiled=True),
        lax.all_gather(qkv_bias, "shard", axis=0, tiled=True),
        lax.all_gather(dense_weight, "shard", axis=0, tiled=True),
        lax.all_gather(dense_bias, "shard", axis=0, tiled=True),
        lax.all_gather(up_weight, "shard", axis=0, tiled=True),
        lax.all_gather(up_bias, "shard", axis=0, tiled=True),
        lax.all_gather(down_weight, "shard", axis=0, tiled=True),
        lax.all_gather(down_bias, "shard", axis=0, tiled=True),
    )
    (
        gain_one,
        shift_one,
        gain_two,
        shift_two,
        qkv_full,
        qkv_add,
        dense_full,
        dense_add,
        up_full,
        up_add,
        down_full,
        down_add,
    ) = gathered
    row_ids = lax.all_gather(segment_ids, "shard", axis=0, tiled=True)
    row_length = row_ids.shape[0]
    places = own * local_rows + jnp.arange(local_rows, dtype=jnp.int32)
    starts = jnp.sum((row_ids[None, :] < segment_ids[:, None]).astype(jnp.int32), axis=1)
    positions = (places - starts).astype(jnp.float32)
    cosine, sine = angle_tables(positions, size // 4)
    hidden = hidden_in.astype(jnp.float32)
    gain_first = gain_one.astype(jnp.float32)
    shift_first = shift_one.astype(jnp.float32)
    gain_second = gain_two.astype(jnp.float32)
    shift_second = shift_two.astype(jnp.float32)
    normed1 = layer_norm(hidden, gain_first, shift_first).astype(jnp.bfloat16)
    normed2 = layer_norm(hidden, gain_second, shift_second).astype(jnp.bfloat16)
    mixed = jnp.dot(normed1, qkv_full, preferred_element_type=jnp.float32) + qkv_add.astype(
        jnp.float32
    )
    query_pre = mixed[:, :width].reshape(local_rows, HEADS, size)
    key_pre = mixed[:, width : 2 * width].reshape(local_rows, HEADS, size)
    queries = rotate(query_pre, cosine, sine).astype(jnp.bfloat16)
    keys_local = rotate(key_pre, cosine, sine).astype(jnp.bfloat16)
    values_local = mixed[:, 2 * width :].reshape(local_rows, HEADS, size).astype(jnp.bfloat16)
    keys_row, values_row = (
        lax.all_gather(keys_local, "shard", axis=0, tiled=True),
        lax.all_gather(values_local, "shard", axis=0, tiled=True),
    )
    key_places = jnp.arange(row_length, dtype=jnp.int32)
    allowed = (row_ids[None, :] == segment_ids[:, None]) & (key_places[None, :] <= places[:, None])
    scale = size ** (-0.5)

    def scores_of():
        raw = (
            jnp.einsum("qhd,khd->hqk", queries, keys_row, preferred_element_type=jnp.float32)
            * scale
        )
        return jnp.where(allowed[None], raw, -1000000000.0)

    scores = scores_of()
    highest = jnp.max(scores, axis=-1, keepdims=True)
    log_total = highest + jnp.log(jnp.sum(jnp.exp(scores - highest), axis=-1, keepdims=True))
    probs = jnp.exp(scores - log_total).astype(jnp.bfloat16)
    context = jnp.einsum("hqk,khd->qhd", probs, values_row, preferred_element_type=jnp.float32)
    context = context.reshape(local_rows, width).astype(jnp.bfloat16)
    attended = jnp.dot(context, dense_full, preferred_element_type=jnp.float32) + dense_add.astype(
        jnp.float32
    )
    gate = jnp.dot(normed2, up_full, preferred_element_type=jnp.float32) + up_add.astype(
        jnp.float32
    )
    active = jax.nn.gelu(gate, approximate=False).astype(jnp.bfloat16)
    output = (
        hidden
        + attended
        + jnp.dot(active, down_full, preferred_element_type=jnp.float32)
        + down_add.astype(jnp.float32)
    ).astype(jnp.bfloat16)
    qkv_back, dense_back, up_back, down_back = (qkv_full, dense_full, up_full, down_full)
    cotangent = out_grad.astype(jnp.float32)
    column_sums = jnp.sum(cotangent, axis=0)
    out_owned = (
        lax.psum_scatter(inner_rows(active, out_grad), "shard", scatter_dimension=0, tiled=True),
        lax.psum_scatter(column_sums, "shard", scatter_dimension=0, tiled=True),
        lax.psum_scatter(inner_rows(context, out_grad), "shard", scatter_dimension=0, tiled=True),
        lax.psum_scatter(column_sums, "shard", scatter_dimension=0, tiled=True),
    )
    active_grad = against(out_grad, down_back)
    gelu_value, gelu_back = jax.vjp(partial(jax.nn.gelu, approximate=False), gate)
    gate_grad = gelu_back(active_grad)[0].astype(jnp.bfloat16)
    normed2_grad = against(gate_grad, up_back)
    norm_value, norm_back_two = jax.vjp(layer_norm, hidden, gain_second, shift_second)
    input_two, gain_two_grad, shift_two_grad = norm_back_two(normed2_grad)
    in_owned = (
        lax.psum_scatter(inner_rows(normed2, gate_grad), "shard", scatter_dimension=0, tiled=True),
        lax.psum_scatter(
            jnp.sum(gate_grad.astype(jnp.float32), axis=0), "shard", scatter_dimension=0, tiled=True
        ),
        lax.psum_scatter(gain_two_grad, "shard", scatter_dimension=0, tiled=True),
        lax.psum_scatter(shift_two_grad, "shard", scatter_dimension=0, tiled=True),
    )
    context_grad = (
        against(out_grad, dense_back).astype(jnp.bfloat16).reshape(local_rows, HEADS, size)
    )
    probs_grad = jnp.einsum(
        "qhd,khd->hqk", context_grad, values_row, preferred_element_type=jnp.float32
    )
    soft = jnp.exp(scores_of() - log_total)
    centered = probs_grad - jnp.sum(soft * probs_grad, axis=-1, keepdims=True)
    score_grad = (soft * centered).astype(jnp.bfloat16)
    query_grad = (
        jnp.einsum("hqk,khd->qhd", score_grad, keys_row, preferred_element_type=jnp.float32) * scale
    )
    key_part = (
        jnp.einsum("hqk,qhd->khd", score_grad, queries, preferred_element_type=jnp.float32) * scale
    )
    value_part = jnp.einsum("hqk,qhd->khd", probs, context_grad, preferred_element_type=jnp.float32)
    key_grad, value_grad = (
        lax.psum_scatter(key_part, "shard", scatter_dimension=0, tiled=True),
        lax.psum_scatter(value_part, "shard", scatter_dimension=0, tiled=True),
    )

    def turn(tensor):
        return rotate(tensor, cosine, sine)

    turned_value, turn_back = jax.vjp(turn, query_pre)
    mixed_grad = jnp.concatenate(
        [
            turn_back(query_grad)[0].reshape(local_rows, width),
            turn_back(key_grad)[0].reshape(local_rows, width),
            value_grad.reshape(local_rows, width),
        ],
        axis=1,
    ).astype(jnp.bfloat16)
    normed1_grad = against(mixed_grad, qkv_back)
    norm_first, norm_back_one = jax.vjp(layer_norm, hidden, gain_first, shift_first)
    input_one, gain_one_grad, shift_one_grad = norm_back_one(normed1_grad)
    attn_owned = (
        lax.psum_scatter(inner_rows(normed1, mixed_grad), "shard", scatter_dimension=0, tiled=True),
        lax.psum_scatter(
            jnp.sum(mixed_grad.astype(jnp.float32), axis=0),
            "shard",
            scatter_dimension=0,
            tiled=True,
        ),
        lax.psum_scatter(gain_one_grad, "shard", scatter_dimension=0, tiled=True),
        lax.psum_scatter(shift_one_grad, "shard", scatter_dimension=0, tiled=True),
    )
    summed = lax.psum(
        (
            out_owned[0],
            out_owned[1],
            out_owned[2],
            out_owned[3],
            in_owned[0],
            in_owned[1],
            in_owned[2],
            in_owned[3],
            attn_owned[0],
            attn_owned[1],
            attn_owned[2],
            attn_owned[3],
        ),
        "rep",
    )
    out_owned = summed[0:4]
    in_owned = summed[4:8]
    attn_owned = summed[8:12]
    input_grad = (cotangent + input_one + input_two).astype(jnp.bfloat16)
    return (
        output,
        input_grad,
        attn_owned[2],
        attn_owned[3],
        in_owned[2],
        in_owned[3],
        attn_owned[0],
        attn_owned[1],
        out_owned[2],
        out_owned[3],
        in_owned[0],
        in_owned[1],
        out_owned[0],
        out_owned[1],
    )


def solution(mesh):
    placed = (
        P(("rep", "shard"), None),
        P(("rep", "shard"), None),
        P(("rep", "shard")),
        P("shard"),
        P("shard"),
        P("shard"),
        P("shard"),
        P("shard", None),
        P("shard"),
        P("shard", None),
        P("shard"),
        P("shard", None),
        P("shard"),
        P("shard", None),
        P("shard"),
    )
    return jax.shard_map(
        shards,
        mesh=mesh,
        in_specs=placed,
        out_specs=(
            P(("rep", "shard"), None),
            P(("rep", "shard"), None),
            P("shard"),
            P("shard"),
            P("shard"),
            P("shard"),
            P("shard", None),
            P("shard"),
            P("shard", None),
            P("shard"),
            P("shard", None),
            P("shard"),
            P("shard", None),
            P("shard"),
        ),
        check_vma=False,
    )
```

profile of v0, /device:TPU:1, one launch (start us, length us, event | category | flops | bytes accessed | tf_op | source)
XLA Modules:
  0.0 2014.2 jit_solution(4458761528023505278)
XLA Ops:
  9.4 22.0 %all-gather.2 = bf16[8,1,384]{2,1,0:T(2,128)(2,1)S(1)} all-gather(bf16[1,1,384]{2,1,0:T(2,128)(2,1)S(1)} %reshape.241), channel_id=1, replica_groups=mesh['rep'=16,'shard'=8] {'shard'}, dimensions={0}, use_global_device_ids=true | all-gather | bytes 6912 | tf_op jit(solution)/shard_map/all_gather | solution.py:72
  31.4 14.5 all-gather.1
  45.9 12.6 all-gather
  58.6 14.0 all-gather.3
  75.8 66.8 %all-gather.16.cloned.1.call-done = bf16[1024,3072]{1,0:T(8,128)(2,1)} async-done(((bf16[128,3072]{1,0:T(8,128)(2,1)}), bf16[1024,3072]{1,0:T(8,128)(2,1)}) %all-gather.16.cloned.1.call-update) | async-done | bytes 6291472 | tf_op jit(solution)/shard_map/all_gather | solution.py:71
  150.4 46.7 %all-gather.22.cloned.1.call-done = bf16[1024,1024]{1,0:T(8,128)(2,1)} async-done(((bf16[128,1024]{1,0:T(8,128)(2,1)}), bf16[1024,1024]{1,0:T(8,128)(2,1)}) %all-gather.22.cloned.1.call-update) | async-done | bytes 2097168 | tf_op jit(solution)/shard_map/all_gather | solution.py:73
  199.7 49.0 %all-gather.20.cloned.1.call-done = bf16[1024,16,64]{0,2,1:T(8,128)(2,1)} async-done(((bf16[128,16,64]{0,2,1:T(8,128)(2,1)}), bf16[1024,16,64]{0,2,1:T(8,128)(2,1)}) %all-gather.20.cloned.1.call-update) | async-done | bytes 2097168 | tf_op jit(solution)/shard_map/all_gather | solution.py:116
  259.4 43.4 %all-gather.18.cloned.1.call-done = bf16[1024,16,64]{0,2,1:T(8,128)(2,1)} async-done(((bf16[128,16,64]{0,2,1:T(8,128)(2,1)}), bf16[1024,16,64]{0,2,1:T(8,128)(2,1)}) %all-gather.18.cloned.1.call-update) | async-done | bytes 2097168 | tf_op jit(solution)/shard_map/all_gather | solution.py:117
  302.8 7.5 multiply_reduce_fusion
  317.3 6.2 convolution_convert_fusion.1
  326.9 21.7 %all-gather.7 = bf16[8,1,512]{2,1,0:T(2,128)(2,1)S(1)} all-gather(bf16[1,1,512]{2,1,0:T(2,128)(2,1)S(1)} %reshape.251), channel_id=1, replica_groups=mesh['rep'=16,'shard'=8] {'shard'}, dimensions={0}, use_global_device_ids=true | all-gather | bytes 9216 | tf_op jit(solution)/shard_map/all_gather | solution.py:76
  348.6 13.7 all-gather.6
  362.4 13.4 all-gather.5
  375.8 99.3 %all-gather.24.cloned.1.call-done = bf16[1024,4096]{1,0:T(8,128)(2,1)} async-done(((bf16[128,4096]{1,0:T(8,128)(2,1)}), bf16[1024,4096]{1,0:T(8,128)(2,1)}) %all-gather.24.cloned.1.call-update) | async-done | bytes 8388624 | tf_op jit(solution)/shard_map/all_gather | solution.py:75
  479.9 166.1 %all-gather.26.cloned.1.call-done = bf16[4096,1024]{1,0:T(8,128)(2,1)} async-done(((bf16[512,1024]{1,0:T(8,128)(2,1)}), bf16[4096,1024]{1,0:T(8,128)(2,1)}) %all-gather.26.cloned.1.call-update) | async-done | bytes 8388624 | tf_op jit(solution)/shard_map/all_gather | solution.py:77
  646.0 10.4 convert_reduce_fusion
  657.4 8.2 fusion.51
  667.5 8.1 fusion.69
  681.8 59.0 %reduce-scatter.9.cloned.1.call-done = f32[128,16,64]{0,2,1:T(8,128)} async-done(((f32[1024,16,64]{0,2,1:T(8,128)}), f32[128,16,64]{0,2,1:T(8,128)}) %reduce-scatter.9.cloned.1.call-update) | async-done | bytes 524304 | tf_op jit(solution)/shard_map/reduce_scatter | solution.py:190
  741.9 92.6 %reduce-scatter.7.cloned.1.call-done = f32[128,16,64]{0,2,1:T(8,128)} async-done(((f32[1024,16,64]{0,2,1:T(8,128)}), f32[128,16,64]{0,2,1:T(8,128)}) %reduce-scatter.7.cloned.1.call-update) | async-done | bytes 524304 | tf_op jit(solution)/shard_map/reduce_scatter | solution.py:189
  836.7 6.4 fusion.54
  843.2 85.0 %reduce-scatter.13.cloned.1.call-done = f32[128,1024]{1,0:T(8,128)} async-done(((f32[1024,1024]{1,0:T(8,128)}), f32[128,1024]{1,0:T(8,128)}) %reduce-scatter.13.cloned.1.call-update) | async-done | bytes 524304 | tf_op jit(solution)/shard_map/reduce_scatter | solution.py:155
  928.2 328.8 %reduce-scatter.15.cloned.1.call-done = f32[128,4096]{1,0:T(8,128)} async-done(((f32[1024,4096]{1,0:T(8,128)}), f32[128,4096]{1,0:T(8,128)}) %reduce-scatter.15.cloned.1.call-update) | async-done | bytes 2097168 | tf_op jit(solution)/shard_map/reduce_scatter | solution.py:165
  1257.0 330.0 %reduce-scatter.17.cloned.1.call-done = f32[512,1024]{1,0:T(8,128)} async-done(((f32[4096,1024]{1,0:T(8,128)}), f32[512,1024]{1,0:T(8,128)}) %reduce-scatter.17.cloned.1.call-update) | async-done | bytes 2097168 | tf_op jit(solution)/shard_map/reduce_scatter | solution.py:153
  1587.0 251.4 %reduce-scatter.11.cloned.1.call-done = f32[128,3072]{1,0:T(8,128)} async-done(((f32[1024,3072]{1,0:T(8,128)}), f32[128,3072]{1,0:T(8,128)}) %reduce-scatter.11.cloned.1.call-update) | async-done | bytes 1572880 | tf_op jit(solution)/shard_map/reduce_scatter | solution.py:209
  1839.1 13.5 all-gather.8
  1852.6 12.3 all-gather.4
  1873.6 6.3 fusion.67
  1880.3 5.3 fusion.61
  1887.2 28.5 %all-reduce.17 = (f32[1024]{0:T(1024)S(1)}, f32[1024]{0:T(1024)S(1)}, f32[1024]{0:T(1024)S(1)}, f32[1024]{0:T(1024)S(1)}, f32[3072]{0:T(1024)S(1)}, /*index=5*/f32[1024]{0:T(1024)S(1)}, f32[4096]{0:T(1024)S(1)}) all-reduce(f32[1024]{0:T(1024)S(1)} %get-tuple-element.23, ...), channel_id=4, replica_groups=mesh['rep'=16,'shard'=8] {'shard'}, use_global_device_ids=true, to_apply=%region_13.14.clone | all-reduce | flops 12288 | bytes 98304
  1916.2 46.1 %all-reduce.15 = (f32[128]{0:T(128)}, f32[128]{0:T(128)}, f32[128]{0:T(128)}, f32[128]{0:T(128)}, f32[384]{0:T(512)}, /*index=5*/f32[128]{0:T(128)S(1)}, f32[512]{0:T(512)}) all-reduce(f32[128]{0:T(128)S(1)} %dynamic-slice.1, f32[128]{0:T(128)S(1)} %dynamic-slice.3, ...), channel_id=1, replica_groups=mesh['rep'=16,'shard'=8] {'rep'}, use_global_device_ids=true, to_apply=%region_14.15 | all-reduce | flops 1536 | bytes 12288 | tf_op jit(solution)/shard_map/psum | solution.py:219
  1962.3 37.0 %all-reduce.20.cloned.1.call-done = (f32[128,3072]{1,0:T(8,128)}, f32[128,1024]{1,0:T(8,128)}, f32[128,4096]{1,0:T(8,128)}, f32[512,1024]{1,0:T(8,128)}) async-done(((f32[128,3072]{1,0:T(8,128)}, f32[128,1024]{1,0:T(8,128)}, f32[128,4096]{1,0:T(8,128)}, f32[512,1024]{1,0:T(8,128)}), (f32[128,3072]{1,0:T(8,128)}, f32[128,1024]{1,0:T(8,128)}, f32[128,4096]{1,0:T(8,128)}, ...) | async-done | bytes 6291472 | tf_op jit(solution)/shard_map/psum | solution.py:219
  (157 shorter events, 71.5 us)
Async XLA Ops:
  7.2 135.4 %all-gather.16.cloned.1.call-start = ((), (), s32[]{:S(2)}) async-start(), calls=%async_computation.6 | async-start | bytes 7077888 | tf_op jit(solution)/shard_map/all_gather | solution.py:71
  7.9 189.2 %all-gather.22.cloned.1.call-start = ((), (), s32[]{:S(2)}) async-start(), calls=%async_computation.9 | async-start | bytes 2359296 | tf_op jit(solution)/shard_map/all_gather | solution.py:73
  8.7 240.1 %all-gather.20.cloned.1.call-start = ((), (), s32[]{:S(2)}) async-start(), calls=%async_computation.8 | async-start | bytes 2359296 | tf_op jit(solution)/shard_map/all_gather | solution.py:116
  147.2 3.0 copy-start.19
  147.2 49.9 %copy-start.6 = (bf16[128,1024]{1,0:T(8,128)(2,1)S(1)}, bf16[128,1024]{1,0:T(8,128)(2,1)}, u32[]{:S(2)}) copy-start(bf16[128,1024]{1,0:T(8,128)(2,1)} %param.16) | copy-start | bytes 786436
  148.0 154.8 %all-gather.18.cloned.1.call-start = ((), (), s32[]{:S(2)}) async-start(), calls=%async_computation.7 | async-start | bytes 2359296 | tf_op jit(solution)/shard_map/all_gather | solution.py:117
  148.9 326.1 %all-gather.24.cloned.1.call-start = ((), (), s32[]{:S(2)}) async-start(), calls=%async_computation.10 | async-start | bytes 9437184 | tf_op jit(solution)/shard_map/all_gather | solution.py:75
  149.5 496.5 %all-gather.26.cloned.1.call-start = ((), (), s32[]{:S(2)}) async-start(), calls=%async_computation.11 | async-start | bytes 9437184 | tf_op jit(solution)/shard_map/all_gather | solution.py:77
  150.1 590.7 %reduce-scatter.9.cloned.1.call-start = ((), (), s32[]{:S(2)}) async-start(), calls=%async_computation.13 | async-start | bytes 4718592 | tf_op jit(solution)/shard_map/reduce_scatter | solution.py:190
  251.9 3.2 copy-start
  259.2 575.3 %reduce-scatter.7.cloned.1.call-start = ((), (), s32[]{:S(2)}) async-start(), calls=%async_computation.12 | async-start | bytes 4718592 | tf_op jit(solution)/shard_map/reduce_scatter | solution.py:189
  302.8 7.5 copy-start.1
  317.3 610.9 %reduce-scatter.13.cloned.1.call-start = ((), (), s32[]{:S(2)}) async-start(), calls=%async_computation.15 | async-start | bytes 4718592 | tf_op jit(solution)/shard_map/reduce_scatter | solution.py:155
  323.5 2.8 copy-start.16
  326.3 22.4 %copy-start.21 = (bf16[128]{0:T(256)(128)(2,1)S(1)}, bf16[128]{0:T(256)(128)(2,1)}, u32[]{:S(2)}) copy-start(bf16[128]{0:T(256)(128)(2,1)} %param.21) | copy-start | bytes 772
  326.3 36.1 %copy-start.22 = (bf16[128]{0:T(256)(128)(2,1)S(1)}, bf16[128]{0:T(256)(128)(2,1)}, u32[]{:S(2)}) copy-start(bf16[128]{0:T(256)(128)(2,1)} %param.20) | copy-start | bytes 772
  326.3 148.8 %copy-start.3 = (bf16[128,1024]{1,0:T(8,128)(2,1)S(1)}, bf16[128,1024]{1,0:T(8,128)(2,1)}, u32[]{:S(2)}) copy-start(bf16[128,1024]{1,0:T(8,128)(2,1)} %param.15) | copy-start | bytes 786436
  326.3 930.7 %reduce-scatter.15.cloned.1.call-start = ((), (), s32[]{:S(2)}) async-start(), calls=%async_computation.16 | async-start | bytes 18874368 | tf_op jit(solution)/shard_map/reduce_scatter | solution.py:165
  475.1 170.9 %copy-start.7 = (bf16[128,1024]{1,0:T(8,128)(2,1)S(1)}, bf16[128,1024]{1,0:T(8,128)(2,1)}, u32[]{:S(2)}) copy-start(bf16[128,1024]{1,0:T(8,128)(2,1)} %param.16) | copy-start | bytes 786436
  665.6 921.4 %reduce-scatter.17.cloned.1.call-start = ((), (), s32[]{:S(2)}) async-start(), calls=%async_computation.17 | async-start | bytes 18874368 | tf_op jit(solution)/shard_map/reduce_scatter | solution.py:153
  675.7 1162.8 %reduce-scatter.11.cloned.1.call-start = ((), (), s32[]{:S(2)}) async-start(), calls=%async_computation.14 | async-start | bytes 14155776 | tf_op jit(solution)/shard_map/reduce_scatter | solution.py:209
  681.8 153.8 %copy-start.13 = (f32[128,16,64]{0,2,1:T(8,128)S(1)}, f32[128,16,64]{0,2,1:T(8,128)}, u32[]{:S(2)}) copy-start(f32[128,16,64]{0,2,1:T(8,128)} %copy-done.12) | copy-start | bytes 1572868
  681.8 154.8 %slice-start = ((f32[128,16,64]{0,2,1:T(8,128)}), f32[128,16,48]{0,2,1:T(8,128)S(1)}, s32[]{:S(2)}) async-start(f32[128,16,64]{0,2,1:T(8,128)} %copy-done.12), calls=%async_computation.19 | async-start | bytes 786432 | tf_op jit(solution)/shard_map/transpose(jvp())/split | solution.py:30
  843.1 1156.2 %all-reduce.20.cloned.1.call-start = ((), (), s32[]{:S(2)}) async-start(), calls=%async_computation.18 | async-start | bytes 12582912 | tf_op jit(solution)/shard_map/psum | solution.py:219
  1838.4 14.1 copy-start.24
  1838.4 26.5 %copy-start.26 = (u32[128]{0:T(128)S(1)}, u32[128]{0:T(128)}, u32[]{:S(2)}) copy-start(u32[128]{0:T(128)} %constant.115) | copy-start | bytes 1540
  1867.4 4.9 copy-start.4
  1867.4 4.9 copy-start.17
  1880.2 5.8 copy-start.9
  1962.3 41.2 %copy-start.25 = (f32[128]{0:T(128)}, f32[128]{0:T(128)S(1)}, u32[]{:S(2)}) copy-start(f32[128]{0:T(128)S(1)} %get-tuple-element.113) | copy-start | bytes 1540
  1999.4 3.4 copy-start.18
  1999.9 3.7 copy-start.15
  (10 other events, 14.2 us)
Sparse Core Ops, SparseCore 0:
  9.7 132.8 all-gather.15
  144.2 52.8 all-gather.21
  199.2 49.4 all-gather.19
  250.7 52.0 all-gather.17
  304.3 170.7 all-gather.23
  476.6 169.3 all-gather.25
  648.4 92.3 reduce-scatter.8
  743.2 91.2 reduce-scatter.6
  836.9 91.2 reduce-scatter.12
  930.5 326.4 reduce-scatter.14
  1259.5 327.4 reduce-scatter.16
  1589.3 249.1 reduce-scatter.10
  1841.2 158.0 all-reduce.19
where the time goes:
time: 2020 us; the launch traced here: 2010 us
  waiting for transfers between devices  1660 us (82%)
  blocking collectives  212 us (10%)
  matrix products  92.1 us (5%)
    reduce_scatter x1, waiting for transfers between devices, shards(): lax.psum_scatter(inner_rows(active, out_grad), 'shard', scatter_dimension...  330 us
    reduce_scatter x1, waiting for transfers between devices, shards(): lax.psum_scatter(inner_rows(normed2, gate_grad), 'shard', scatter_dimensi...  329 us
    reduce_scatter x1, waiting for transfers between devices, shards(): lax.psum_scatter(inner_rows(normed1, mixed_grad), 'shard', scatter_dimens...  251 us
    all_gather x1, waiting for transfers between devices, shards(): lax.all_gather(down_weight, 'shard', axis=0, tiled=True)  166 us
    all_gather x1, waiting for transfers between devices, shards(): lax.all_gather(up_weight, 'shard', axis=0, tiled=True)  99.3 us
    reduce_scatter x1, waiting for transfers between devices, shards(): lax.psum_scatter(key_part, 'shard', scatter_dimension=0, tiled=True)  92.6 us
    reduce_scatter x1, waiting for transfers between devices, shards(): lax.psum_scatter(inner_rows(context, out_grad), 'shard', scatter_dimensio...  85 us
    all_gather x1, waiting for transfers between devices, shards(): lax.all_gather(qkv_weight, 'shard', axis=0, tiled=True)  66.8 us
  transfers between devices with their start and end apart: 13, of which 13 were waited for; matrix products, arithmetic and copies ran while one was open for 6% of the time, Pallas kernels for 0%

commit v1 on v0

v1 whole, which is shorter than its diff:
```python
import functools

import jax
import jax.numpy as jnp
from jax import lax
from jax.experimental import pallas as pl
from jax.experimental.pallas import tpu as pltpu
from jax.sharding import PartitionSpec as P

BF = jnp.bfloat16
F32 = jnp.float32
MESH = pl.DeviceIdType.MESH
SEMS = 176


def flip(value, mask):
    out = value
    bit = 1
    while bit <= mask:
        if mask & bit:
            out = out + bit - 2 * bit * lax.rem(lax.div(value, bit), 2)
        bit *= 2
    return out


def nt(left, right):
    return lax.dot_general(left, right, (((1,), (1,)), ((), ())), preferred_element_type=F32)


def nn(left, right):
    return jnp.dot(left, right, preferred_element_type=F32)


def fold(block):
    return jnp.sum(block.reshape(block.shape[0] // 8, 8, block.shape[1]), axis=0)


def kernel(
    hid_ref, g_ref, seg_ref, pack_ref, wqkv_ref, wup_ref, wdense_ref, wdown_ref,
    out_ref, ing_ref, f1_ref, f2_ref, f3_ref, gvec_ref,
    HB, GB, SG, PK, WQ, WU, VEC, B24, XH, N1, N2, QKP, TAB, START, QTM, QM, KT, K, V, VT,
    GP, ACT, ACTT, PT, CTXT, CTX, DCM, DCTM, DG, DGT, DQT, DK, DV, M, MT,
    PB, PRA, PRB, PRX, PRZ, PTX, PUB, DB, DRA, DRB, DRX, DRZ, DTX, DUB, ACC,
    G1, X1, C1, R1, S1, G2, X2, C2, R2, S2, A2, G3, X3, C3, R3, S3, A3,
    SUMS, CG, CDG, SV, SVR, LV, LVX, LC, LCR,
    ssem, rsem, lsem,
):
    r = lax.axis_index("rep")
    s = lax.axis_index("shard")
    c = lax.rem(r, 2)
    chip = lax.div(r, 2)
    z = lax.div(s, 2)
    l = lax.rem(s, 2)
    other = 1 - l
    half = lax.rem(c + s, 2)

    def shard_to(k):
        return {"shard": flip(s, k)}

    def chip_to(k):
        return {"rep": flip(chip, k) * 2 + c}

    partner = {"rep": chip * 2 + 1 - c}
    zk = [None] + [flip(z, k) for k in (1, 2, 3)]

    barrier = pltpu.get_barrier_semaphore()
    peers = [shard_to(k) for k in range(1, 8)] + [chip_to(k) for k in range(1, 8)] + [partner]
    for peer in peers:
        pl.semaphore_signal(barrier, inc=1, device_id=peer, device_id_type=MESH)
    pl.semaphore_wait(barrier, len(peers))

    used = [0]
    sent = []

    def remote(src, dst, device):
        at = used[0]
        used[0] += 1
        copy = pltpu.make_async_remote_copy(
            src_ref=src, dst_ref=dst, send_sem=ssem.at[at], recv_sem=rsem.at[at],
            device_id=device, device_id_type=MESH,
        )
        copy.start()
        sent.append(copy)
        return copy

    def lanes(start, size):
        return pl.ds(pl.multiple_of(start, 128), size)

    def rows(start, size):
        return pl.ds(pl.multiple_of(start, 16), size)

    def gather_start(x_ref, XB):
        first = remote(x_ref.at[0:64], XB.at[z, l, 0:64], shard_to(1))
        whole = [remote(x_ref, XB.at[z, l], shard_to(2 * k)) for k in (1, 3, 2)]
        last = remote(x_ref.at[64:128], XB.at[z, l, 64:128], shard_to(1))
        return XB, first, whole, last

    def gather_forward(state):
        XB, first, whole, last = state
        first.wait_recv()
        rest = [last]
        for k in (1, 3, 2):
            rest.append(remote(XB.at[z, other, 0:64], XB.at[z, other, 0:64], shard_to(2 * k)))
        for copy, k in zip(whole, (1, 3, 2)):
            copy.wait_recv()
            rest.append(remote(XB.at[zk[k], l, 64:128], XB.at[zk[k], l, 64:128], shard_to(1)))
        return rest

    def arrived(copies):
        for copy in copies:
            copy.wait_recv()

    small = [remote(pack_ref, PK.at[s], shard_to(k)) for k in range(1, 8)]
    small += [remote(seg_ref, SG.at[s], shard_to(k)) for k in range(1, 8)]
    part = rows(64 * c, 64)
    gather_h = gather_start(hid_ref, HB)
    weights = []
    for k in range(1, 8):
        sp = flip(s, k)
        for j in range(3):
            weights.append(remote(
                wqkv_ref.at[part, lanes(1024 * j + 128 * sp, 128)],
                WQ.at[s, part, 128 * j : 128 * j + 128], shard_to(k)))
        weights.append(remote(wup_ref.at[part, lanes(512 * sp, 512)], WU.at[s, part], shard_to(k)))
    local = []
    for j in range(3):
        local.append(pltpu.make_async_copy(
            wqkv_ref.at[part, lanes(1024 * j + 128 * s, 128)],
            WQ.at[s, part, 128 * j : 128 * j + 128], lsem.at[j]))
    local.append(pltpu.make_async_copy(wup_ref.at[part, lanes(512 * s, 512)], WU.at[s, part], lsem.at[3]))
    for copy in local:
        copy.start()
    HB[z, l] = hid_ref[...]
    GB[z, l] = g_ref[...]
    PK[s] = pack_ref[...]
    SG[s] = seg_ref[...]
    rest_h = gather_forward(gather_h)
    for copy in local:
        copy.wait()
    arrived(weights)
    across = [remote(WQ.at[:, part], WQ.at[:, part], partner), remote(WU.at[:, part], WU.at[:, part], partner)]
    gather_g = gather_start(g_ref, GB)

    arrived(small)
    for sp in range(8):
        block = PK[sp].astype(F32)
        at = slice(128 * sp, 128 * sp + 128)
        for j in range(4):
            VEC[j : j + 1, at] = block[j : j + 1]
        VEC[4:5, at] = block[7:8] + block[12:13]
        B24[3 * sp : 3 * sp + 3] = block[4:7]
    own = PK[s].astype(F32)
    bias_up = jnp.concatenate([own[8 + j : 9 + j] for j in range(4)], axis=1)
    bias_q = jnp.concatenate([B24[pl.ds(8 * j + s, 1)] for j in range(3)], axis=1)
    own_bias = own[7:8] + own[12:13]
    del own_bias
    seg_row = jnp.concatenate([SG[sp, 0:1] for sp in range(8)], axis=1).astype(F32)
    count = jnp.zeros((1, 1024), F32)
    for sp in range(8):
        column = jnp.transpose(jnp.broadcast_to(SG[sp, 0:1].astype(F32), (128, 128)))[:, 0:1]
        count = count + jnp.sum((column < seg_row).astype(F32), axis=0, keepdims=True)
    START[...] = jnp.broadcast_to(count.astype(jnp.int32), (8, 1024))
    place = lax.broadcasted_iota(jnp.int32, (8, 1024), 1).astype(F32)
    row8 = lax.broadcasted_iota(jnp.int32, (8, 1024), 0)
    inverse = jnp.zeros((8, 1024), F32)
    for j in range(8):
        inverse = jnp.where(row8 == j, 10000.0 ** (-j / 8.0), inverse)
    angles = (place - count) * inverse
    TAB[0] = jnp.cos(angles)
    TAB[1] = jnp.sin(angles)
    arrived(rest_h)
    arrived(across)

    gain1, shift1, gain2, shift2 = (VEC[j : j + 1] for j in range(4))

    @pl.loop(0, 4)
    def _(i):
        at = rows(256 * i, 256)
        cols = lanes(256 * i, 256)
        block = HB[i].reshape(256, 1024).astype(F32)
        center = block - jnp.mean(block, axis=-1, keepdims=True)
        spread = jnp.mean(center * center, axis=-1, keepdims=True)
        xhat = center * lax.rsqrt(spread + 1e-05)
        XH[at] = xhat.astype(BF)
        n1 = (xhat * gain1 + shift1).astype(BF)
        n2 = (xhat * gain2 + shift2).astype(BF)
        N1[at] = n1
        N2[at] = n2
        mixed = nn(n1, WQ[...].reshape(1024, 384)) + bias_q
        QKP[:, cols] = jnp.transpose(mixed[:, :256])
        V[at] = mixed[:, 256:].astype(BF)
        VT[:, cols] = jnp.transpose(mixed[:, 256:]).astype(BF)
        gate = nn(n2, WU[...].reshape(1024, 512)) + bias_up
        phi = 0.5 + 0.5 * lax.erf(gate * 0.7071067811865476)
        GP[at] = phi + gate * jnp.exp(-0.5 * gate * gate) * 0.3989422804014327
        active = gate * phi
        ACT[at] = active.astype(BF)
        ACTT[:, cols] = jnp.transpose(active).astype(BF)

    rest_g = gather_forward(gather_g)

    cosine = TAB[0]
    sine = TAB[1]
    for base in (0, 64, 128, 192):
        one = QKP[base : base + 8]
        two = QKP[base + 8 : base + 16]
        QKP[base : base + 8] = one * cosine - two * sine
        QKP[base + 8 : base + 16] = two * cosine + one * sine
    queries = QKP[0:128].astype(BF).astype(F32) * 0.125
    keys = QKP[128:256]
    low_rows = lax.broadcasted_iota(jnp.int32, (128, 1024), 0) < 64
    low_cols = lax.broadcasted_iota(jnp.int32, (1024, 128), 1) < 64
    QTM[0] = jnp.where(low_rows, queries, 0.0).astype(BF)
    QTM[1] = jnp.where(low_rows, 0.0, queries).astype(BF)
    back = jnp.transpose(queries)
    QM[0] = jnp.where(low_cols, back, 0.0).astype(BF)
    QM[1] = jnp.where(low_cols, 0.0, back).astype(BF)
    KT[...] = keys.astype(BF)
    K[...] = jnp.transpose(keys).astype(BF)

    @pl.loop(0, 2)
    def _(head):
        hr = rows(64 * head, 64)
        for j in range(4):
            top = 256 * (j + 1)
            q = slice(256 * j, 256 * j + 256)
            scores = nn(K[0:top], QTM[head, :, q])
            ki = lax.broadcasted_iota(jnp.int32, (top, 256), 0)
            qi = lax.broadcasted_iota(jnp.int32, (top, 256), 1) + 256 * j
            allowed = (ki <= qi) & (ki >= START[0:1, q])
            scores = jnp.where(allowed, scores, -1e9)
            weight = jnp.exp(scores - jnp.max(scores, axis=0, keepdims=True))
            probs = (weight * (1.0 / jnp.sum(weight, axis=0, keepdims=True))).astype(BF)
            PT[head, 0:top, q] = probs
            CTXT[hr, q] = nn(VT[hr, 0:top], probs).astype(BF)

    CTX[...] = jnp.transpose(CTXT[...].astype(F32)).astype(BF)

    def scatter_start(TB, RA, RB):
        a = [remote(TB.at[zk[k], :, 0:64], RA.at[k - 1], shard_to(2 * k)) for k in (1, 3, 2)]
        b = remote(TB.at[:, other, 64:128], RB, shard_to(1))
        return a, b

    def scatter_middle(state, TB, RA, RB, RX, RZ, TX, UB):
        a, b = state
        arrived(a)
        TX[...] = (
            TB[z, other, 0:64].astype(F32) + RA[0, other].astype(F32)
            + RA[1, other].astype(F32) + RA[2, other].astype(F32)
        ).astype(BF)
        out = [remote(TX, RX, shard_to(1))]
        b.wait_recv()
        for k in (1, 3, 2):
            UB[k - 1] = (TB[zk[k], l, 64:128].astype(F32) + RB[zk[k]].astype(F32)).astype(BF)
            out.append(remote(UB.at[k - 1], RZ.at[k - 1], shard_to(2 * k)))
        return out

    def scatter_end(out, TB, RA, RB, RX, RZ):
        arrived(out)
        ACC[0:64] = (
            TB[z, l, 0:64].astype(F32) + RA[0, l].astype(F32) + RA[1, l].astype(F32)
            + RA[2, l].astype(F32) + RX[...].astype(F32)
        )
        ACC[64:128] = (
            TB[z, l, 64:128].astype(F32) + RB[z].astype(F32) + RZ[0].astype(F32)
            + RZ[1].astype(F32) + RZ[2].astype(F32)
        )

    @pl.loop(0, 4)
    def _(i):
        at = rows(256 * i, 256)
        total = nn(CTX[at], wdense_ref[...]) + nn(ACT[at], wdown_ref[...])
        PB[i] = total.astype(BF).reshape(2, 128, 1024)

    out_state = scatter_start(PB, PRA, PRB)
    arrived(rest_g)

    CG[...] = jnp.zeros_like(CG)
    CDG[...] = jnp.zeros_like(CDG)
    low_256 = lax.broadcasted_iota(jnp.int32, (256, 128), 1) < 64
    low_t256 = lax.broadcasted_iota(jnp.int32, (128, 256), 0) < 64

    @pl.loop(0, 4)
    def _(i):
        at = rows(256 * i, 256)
        cols = lanes(256 * i, 256)
        block = GB[i].reshape(256, 1024)
        CG[...] += fold(block.astype(F32))
        grad = nt(block, wdense_ref[...])
        DCM[0, at] = jnp.where(low_256, grad, 0.0).astype(BF)
        DCM[1, at] = jnp.where(low_256, 0.0, grad).astype(BF)
        turned = jnp.transpose(grad)
        DCTM[0, :, cols] = jnp.where(low_t256, turned, 0.0).astype(BF)
        DCTM[1, :, cols] = jnp.where(low_t256, 0.0, turned).astype(BF)
        gate_grad = (nt(block, wdown_ref[...]) * GP[at]).astype(BF)
        DG[at] = gate_grad
        wide = gate_grad.astype(F32)
        CDG[...] += fold(wide)
        DGT[:, cols] = jnp.transpose(wide).astype(BF)

    mine = half

    def pair_start(GR, X):
        return remote(GR.at[:, lanes(512 * (1 - mine), 512)], X, partner)

    def spread_start(pair, GR, X, C, R, size):
        pair.wait_recv()
        C[...] = (GR[:, lanes(512 * mine, 512)].astype(F32) + X[...].astype(F32)).astype(BF)
        return [
            remote(C.at[rows(size * flip(chip, k), size)], R.at[k - 1], chip_to(k)) for k in range(1, 8)
        ]

    def spread_sum(copies, C, R, S, size):
        arrived(copies)
        total = C[rows(size * chip, size)].astype(F32)
        for k in range(7):
            total = total + R[k].astype(F32)
        S[...] = total.astype(BF)

    grads = GB[...].reshape(1024, 1024)
    G1[0:512] = nn(ACTT[...], grads).astype(BF)
    G1[512:640] = nn(CTXT[...], grads).astype(BF)
    pair1 = pair_start(G1, X1)
    G2[...] = nn(DGT[...], N2[...]).astype(BF)
    pair2 = pair_start(G2, X2)
    spread1 = spread_start(pair1, G1, X1, C1, R1, 80)
    out_rest = scatter_middle(out_state, PB, PRA, PRB, PRX, PRZ, PTX, PUB)
    spread2 = spread_start(pair2, G2, X2, C2, R2, 64)

    DK[...] = jnp.zeros_like(DK)
    DV[...] = jnp.zeros_like(DV)

    @pl.loop(0, 2)
    def _(head):
        hr = rows(64 * head, 64)
        for j in range(4):
            top = 256 * (j + 1)
            q = slice(256 * j, 256 * j + 256)
            probs = PT[head, 0:top, q]
            soft = probs.astype(F32)
            probs_grad = nn(V[0:top], DCTM[head, :, q])
            middle = jnp.sum(soft * probs_grad, axis=0, keepdims=True)
            score_grad = (soft * (probs_grad - middle)).astype(BF)
            DQT[hr, q] = nn(KT[hr, 0:top], score_grad) * 0.125
            DK[0:top] += nn(score_grad, QM[head, q])
            DV[0:top] += nn(probs, DCM[head, q])

    dk = jnp.transpose(DK[...])
    QKP[0:128] = DQT[...]
    QKP[128:256] = dk
    for base in (0, 64, 128, 192):
        one = QKP[base : base + 8]
        two = QKP[base + 8 : base + 16]
        QKP[base : base + 8] = one * cosine + two * sine
        QKP[base + 8 : base + 16] = two * cosine - one * sine
    MT[0:256] = QKP[...].astype(BF)
    MT[256:384] = jnp.transpose(DV[...]).astype(BF)
    M[:, 0:256] = jnp.transpose(QKP[...]).astype(BF)
    M[:, 256:384] = DV[...].astype(BF)
    G3[...] = nn(MT[...], N1[...]).astype(BF)
    pair3 = pair_start(G3, X3)

    SUMS[...] = jnp.zeros_like(SUMS)

    @pl.loop(0, 4)
    def _(i):
        at = rows(256 * i, 256)
        xhat = XH[at].astype(F32)
        one = nt(M[at], WQ[...].reshape(1024, 384))
        two = nt(DG[at], WU[...].reshape(1024, 512))
        DB[i] = (one * gain1 + two * gain2).astype(BF).reshape(2, 128, 1024)
        SUMS[0] += fold(one * xhat)
        SUMS[1] += fold(one)
        SUMS[2] += fold(two * xhat)
        SUMS[3] += fold(two)

    in_state = scatter_start(DB, DRA, DRB)

    SV[...] = jnp.zeros_like(SV)
    bias_grad = jnp.sum(fold(M[...].astype(F32)), axis=0, keepdims=True)
    B24[...] = jnp.zeros_like(B24)
    for j in range(3):
        B24[pl.ds(8 * j + s, 1)] = bias_grad[:, 128 * j : 128 * j + 128]
    for sp in range(8):
        at = slice(128 * sp, 128 * sp + 128)
        for j in range(4):
            SV[sp, j : j + 1] = jnp.sum(SUMS[j, :, at], axis=0, keepdims=True)
        SV[sp, 4:7] = B24[3 * sp : 3 * sp + 3]
    vectors = [remote(SV.at[flip(s, k)], SVR.at[k - 1], shard_to(k)) for k in range(1, 8)]

    spread3 = spread_start(pair3, G3, X3, C3, R3, 48)

    def give(S, out, size):
        at = rows(size * chip, size)
        out[at, lanes(512 * mine, 512)] = S[...]
        return [
            remote(S, out.at[at, lanes(512 * mine, 512)], chip_to(k)) for k in range(1, 8)
        ]

    spread_sum(spread1, C1, R1, S1, 80)
    give1 = give(S1, f1_ref, 80)

    source = lax.rem(lax.div(s, 4) + c, 2)

    def turn(S, A, size):
        base = used[0]
        used[0] += 4
        slot = lax.div(s, 2)

        def descriptor(m, device):
            return pltpu.make_async_remote_copy(
                src_ref=S.at[:, 128 * m : 128 * m + 128], dst_ref=A.at[slot],
                send_sem=ssem.at[base + m], recv_sem=rsem.at[base + slot],
                device_id={"shard": device}, device_id_type=MESH,
            )

        for m in range(4):
            device = 4 * half + m

            @pl.when(device != s)
            def _():
                descriptor(m, device).start()

            @pl.when(device == s)
            def _():
                A[slot] = S[:, 128 * m : 128 * m + 128]

        return base

    def turned(base, S, A, size):
        for m in range(4):
            @pl.when(4 * half + m != s)
            def _():
                pltpu.make_async_remote_copy(
                    src_ref=S.at[:, 128 * m : 128 * m + 128], dst_ref=A.at[m],
                    send_sem=ssem.at[base + m], recv_sem=rsem.at[base + m],
                    device_id={"shard": flip(s, 1)}, device_id_type=MESH,
                ).wait_send()

            @pl.when(2 * m + source != s)
            def _():
                pltpu.make_async_remote_copy(
                    src_ref=S.at[:, 128 * m : 128 * m + 128], dst_ref=A.at[m],
                    send_sem=ssem.at[base + m], recv_sem=rsem.at[base + m],
                    device_id={"shard": flip(s, 1)}, device_id_type=MESH,
                ).wait_recv()

    def give_turned(A, out, size):
        at = rows(size * chip, size)
        out[source, :, at] = A[...]
        return [remote(A, out.at[source, :, at], chip_to(k)) for k in range(1, 8)]

    spread_sum(spread2, C2, R2, S2, 64)
    turn2 = turn(S2, A2, 64)
    out_end = out_rest
    scatter_end(out_end, PB, PRA, PRB, PRX, PRZ)
    out_ref[...] = (hid_ref[...].astype(F32) + ACC[...] + VEC[4:5]).astype(BF)

    in_rest = scatter_middle(in_state, DB, DRA, DRB, DRX, DRZ, DTX, DUB)
    turned(turn2, S2, A2, 64)
    give2 = give_turned(A2, f2_ref, 64)

    spread_sum(spread3, C3, R3, S3, 48)
    turn3 = turn(S3, A3, 48)
    arrived(vectors)
    LV[...] = jnp.zeros_like(LV)
    total = SV[s]
    for k in range(7):
        total = total + SVR[k]
    LV[0:7] = total[0:7]
    up_grad = jnp.sum(CDG[...], axis=0, keepdims=True)
    for j in range(4):
        LV[8 + j : 9 + j] = up_grad[:, 128 * j : 128 * j + 128]
    LV[12:13] = jnp.sum(CG[:, lanes(128 * s, 128)], axis=0, keepdims=True)
    pair_v = remote(LV, LVX, partner)

    turned(turn3, S3, A3, 48)
    give3 = give_turned(A3, f3_ref, 48)
    pair_v.wait_recv()
    LC[...] = LV[...] + LVX[...]
    LCR[chip] = LC[...]
    spread_v = [remote(LC, LCR.at[chip], chip_to(k)) for k in range(1, 8)]

    arrived(give1)
    last1 = remote(f1_ref.at[:, lanes(512 * mine, 512)], f1_ref.at[:, lanes(512 * mine, 512)], partner)
    arrived(give2)
    last2 = remote(f2_ref.at[source], f2_ref.at[source], partner)

    scatter_end(in_rest, DB, DRA, DRB, DRX, DRZ)
    block = hid_ref[...].astype(F32)
    center = block - jnp.mean(block, axis=-1, keepdims=True)
    spread = jnp.mean(center * center, axis=-1, keepdims=True)
    scale = lax.rsqrt(spread + 1e-05)
    xhat = center * scale
    grad = ACC[...]
    grad = grad - jnp.mean(grad, axis=-1, keepdims=True) - xhat * jnp.mean(grad * xhat, axis=-1, keepdims=True)
    ing_ref[...] = (g_ref[...].astype(F32) + scale * grad).astype(BF)

    arrived(spread_v)
    total = LCR[0]
    for k in range(1, 8):
        total = total + LCR[k]
    gvec_ref[...] = total

    arrived(give3)
    last3 = remote(f3_ref.at[source], f3_ref.at[source], partner)
    arrived([last1, last2, last3])
    for copy in sent:
        copy.wait_send()
    assert used[0] <= SEMS, used[0]


def block_call(*args):
    vm = pltpu.VMEM
    scratch = [
        vm((4, 2, 128, 1024), BF), vm((4, 2, 128, 1024), BF), vm((8, 8, 128), jnp.int32), vm((8, 16, 128), BF),
        vm((8, 128, 384), BF), vm((8, 128, 512), BF), vm((8, 1024), F32), vm((24, 128), F32),
        vm((1024, 1024), BF), vm((1024, 1024), BF), vm((1024, 1024), BF), vm((256, 1024), F32),
        vm((2, 8, 1024), F32), vm((8, 1024), jnp.int32),
        vm((2, 128, 1024), BF), vm((2, 1024, 128), BF), vm((128, 1024), BF), vm((1024, 128), BF),
        vm((1024, 128), BF), vm((128, 1024), BF),
        vm((1024, 512), F32), vm((1024, 512), BF), vm((512, 1024), BF), vm((2, 1024, 1024), BF),
        vm((128, 1024), BF), vm((1024, 128), BF), vm((2, 1024, 128), BF), vm((2, 128, 1024), BF),
        vm((1024, 512), BF), vm((512, 1024), BF), vm((128, 1024), F32), vm((1024, 128), F32), vm((1024, 128), F32),
        vm((1024, 384), BF), vm((384, 1024), BF),
    ]
    for _ in range(2):
        scratch += [
            vm((4, 2, 128, 1024), BF), vm((3, 2, 64, 1024), BF), vm((4, 64, 1024), BF), vm((64, 1024), BF),
            vm((3, 64, 1024), BF), vm((64, 1024), BF), vm((3, 64, 1024), BF),
        ]
    scratch += [vm((128, 1024), F32)]
    scratch += [vm((640, 1024), BF), vm((640, 512), BF), vm((640, 512), BF), vm((7, 80, 512), BF), vm((80, 512), BF)]
    for size in (64, 48):
        scratch += [
            vm((8 * size, 1024), BF), vm((8 * size, 512), BF), vm((8 * size, 512), BF), vm((7, size, 512), BF),
            vm((size, 512), BF), vm((4, size, 128), BF),
        ]
    scratch += [
        vm((4, 8, 1024), F32), vm((8, 1024), F32), vm((8, 512), F32), vm((8, 16, 128), F32), vm((7, 16, 128), F32),
        vm((16, 128), F32), vm((16, 128), F32), vm((16, 128), F32), vm((8, 16, 128), F32),
        pltpu.SemaphoreType.DMA((SEMS,)), pltpu.SemaphoreType.DMA((SEMS,)), pltpu.SemaphoreType.DMA((4,)),
    ]
    return pl.pallas_call(
        kernel,
        out_shape=(
            jax.ShapeDtypeStruct((128, 1024), BF), jax.ShapeDtypeStruct((128, 1024), BF),
            jax.ShapeDtypeStruct((640, 1024), BF), jax.ShapeDtypeStruct((2, 4, 512, 128), BF),
            jax.ShapeDtypeStruct((2, 4, 384, 128), BF), jax.ShapeDtypeStruct((16, 128), F32),
        ),
        in_specs=[pl.BlockSpec(memory_space=pltpu.VMEM)] * 8,
        out_specs=[pl.BlockSpec(memory_space=pltpu.VMEM)] * 6,
        scratch_shapes=scratch,
        compiler_params=pltpu.CompilerParams(
            collective_id=0, has_side_effects=True, vmem_limit_bytes=62 * 2**20
        ),
    )(*args)


def shards(
    hidden_in, out_grad, segment_ids, first_gain, first_shift, second_gain, second_shift,
    qkv_weight, qkv_bias, dense_weight, dense_bias, up_weight, up_bias, down_weight, down_bias,
):
    pack = jnp.concatenate([
        first_gain, first_shift, second_gain, second_shift, qkv_bias, dense_bias, up_bias, down_bias,
        jnp.zeros((384,), BF),
    ]).reshape(16, 128)
    seg = jnp.broadcast_to(segment_ids.reshape(1, 128), (8, 128))
    out, ing, first, second, third, vectors = block_call(
        hidden_in, out_grad, seg, pack, qkv_weight, up_weight, dense_weight, down_weight
    )
    third = third.astype(F32).reshape(2, 4, 3, 128, 128)
    grad_qkv = jnp.transpose(third, (4, 2, 1, 0, 3)).reshape(128, 3072)
    grad_up = jnp.transpose(second.astype(F32), (3, 1, 0, 2)).reshape(128, 4096)
    first = first.astype(F32)
    return (
        out, ing, vectors[0], vectors[1], vectors[2], vectors[3],
        grad_qkv, vectors[4:7].reshape(384),
        first[512:640], vectors[12],
        grad_up, vectors[8:12].reshape(512),
        first[0:512], vectors[12],
    )


def solution(mesh):
    both, one, wide = P(("rep", "shard"), None), P("shard"), P("shard", None)
    placed = (
        both, both, P(("rep", "shard")), one, one, one, one, wide, one, wide, one, wide, one, wide, one,
    )
    return jax.shard_map(
        shards, mesh=mesh, in_specs=placed,
        out_specs=(both, both, one, one, one, one, wide, one, wide, one, wide, one, wide, one),
        check_vma=False,
    )
```

time: 2020 us -> 162 us (0.08)
  waiting for transfers between devices: 1660 us -> 0 us
  blocking collectives: 212 us -> 0 us
  Pallas kernels: 0 us -> 135 us
  matrix products: 92.1 us -> 0 us
    reduce_scatter x6 -> x0, waiting for transfers between devices: 1150 us -> none  [the longest x1 330 us: shards(): lax.psum_scatter(inner_rows(active, out_grad), 'shard', scatter_dimension...]
    all_gather x6 -> x0, waiting for transfers between devices: 471 us -> none  [the longest x1 166 us: shards(): lax.all_gather(down_weight, 'shard', axis=0, tiled=True)]
    all_gather x9 -> x0, blocking collectives: 138 us -> none  [the longest x1 22 us: shards(): lax.all_gather(qkv_bias, 'shard', axis=0, tiled=True)]
    pallas_call x0 -> x1, Pallas kernels: none -> 135 us  [block_call(): pl.pallas_call(kernel, out_shape=(jax.ShapeDtypeStruct((128, 1024), BF),...]
    dot_general x18 -> x0, matrix products: 92.1 us -> none  [the longest x4 25.5 us: inner_rows(): lax.dot_general(left, right, (((0,), (0,)), ((), ())), preferred_element_...]
    psum x1 -> x0, blocking collectives: 46.1 us -> none  [shards(): lax.psum((out_owned[0], out_owned[1], out_owned[2], out_owned[3], in_owne...]
    psum x1 -> x0, waiting for transfers between devices: 37 us -> none  [shards(): lax.psum((out_owned[0], out_owned[1], out_owned[2], out_owned[3], in_owne...]
    unnamed x1 -> x0, blocking collectives: 28.5 us -> none
  transfers between devices with their start and end apart: 13 -> 0, of which waited for: 13 -> 0; matrix products, arithmetic and copies ran while one was open for 6% -> 0% of each run, Pallas kernels for 0% -> 0%
where the time goes in v1:
time: 162 us; the launch traced here: 159 us
  Pallas kernels  135 us (83%)
  local copies, waits for them, and re-layouts  22.1 us (14%)
    pallas_call x1, Pallas kernels, block_call(): pl.pallas_call(kernel, out_shape=(jax.ShapeDtypeStruct((128, 1024), BF),...  135 us
    unnamed x26, local copies, waits for them, and re-layouts  11 us
    reshape x2, local copies, waits for them, and re-layouts, shards(): grad_qkv = jnp.transpose(third, (4, 2, 1, 0, 3)).reshape(128, 3072)  3.57 us

profile of v1, /device:TPU:1, one launch (start us, length us, event | category | flops | bytes accessed | tf_op | source)
XLA Modules:
  0.0 159.2 jit_solution(4816814864615951360)
XLA Ops:
  0.6 1.2 broadcast_in_dim.8.seg_ref
  1.9 0.8 dynamic-update-slice
  2.7 0.8 dynamic-update-slice.1
  3.6 0.8 dynamic-update-slice.2
  4.4 0.8 dynamic-update-slice.3
  5.2 0.9 dynamic-update-slice.4
  6.1 0.8 dynamic-update-slice.5
  6.9 0.9 dynamic-update-slice.6
  7.8 0.8 dynamic-update-slice.7
  8.6 0.2 dynamic-update-slice.8
  8.8 0.6 copy-done.5
  9.4 134.9 %shard_map.254 = (bf16[128,1024]{1,0:T(8,128)(2,1)}, bf16[128,1024]{1,0:T(8,128)(2,1)}, bf16[640,1024]{1,0:T(8,128)(2,1)}, bf16[2,4,512,128]{3,2,1,0:T(8,128)(2,...) custom-call(bf16[128,1024]{1,0:T(8,128)(2,1)} %hid_ref.1, bf16[128,1024]{1,0:T(8,128)(2,1)} %g_ref.1, ...), custom_call_target="tpu_custom_call" | custom-call | tf_op jit(solution)/shard_map/pallas_call | solution.py:544
  144.3 1.4 slice_bitcast_fusion.2
  145.7 1.3 convert_bitcast_fusion.1
  147.0 1.2 copy.30
  148.2 0.0 copy-start.4
  148.2 0.0 copy-start.1
  148.2 2.4 %reshape.64 = f32[128,3072]{1,0:T(8,128)} reshape(f32[128,3,4,2,128]{4,3,2,1,0:T(2,128)S(1)} %copy.30) | data formatting | bytes 3145728 | tf_op jit(solution)/shard_map/reshape | solution.py:573
  150.6 0.0 copy-done.4
  150.6 0.6 slice_bitcast_fusion.1
  151.2 1.8 %slice.37 = f32[128,1024]{1,0:T(8,128)} slice(bf16[640,1024]{1,0:T(8,128)(2,1)} %get-tuple-element.24), slice={[512:640], [0:1024]} | slice | bytes 1048576 | tf_op jit(solution)/shard_map/slice | solution.py:579
  153.0 0.0 copy-done.1
  153.0 0.1 convert_bitcast_fusion
  153.1 0.1 copy.31
  153.3 0.0 copy-start
  153.3 1.8 %copy.32 = f32[128,4096]{1,0:T(8,128)} copy(f32[128,4096]{0,1:T(8,128)S(1)} %bitcast.22) | data formatting | bytes 4194304
  155.1 0.6 slice_bitcast_fusion
  155.7 1.6 slice.38
  157.2 0.5 copy.45
  157.8 0.0 copy-done.3
  157.8 0.7 copy.46
  158.5 0.7 copy.47
  (9 shorter events, 0.0 us)
Async XLA Ops:
  8.8 0.6 copy-start.5
  145.7 11.6 %copy-start.6 = (f32[128]{0:T(128)}, f32[128]{0:T(128)S(1)}, u32[]{:S(2)}) copy-start(f32[128]{0:T(128)S(1)} %get-tuple-element.96) | copy-start | bytes 1540
  148.2 2.4 %copy-start.4 = (f32[16,128]{1,0:T(8,128)S(1)}, f32[16,128]{1,0:T(8,128)}, u32[]{:S(2)}) copy-start(f32[16,128]{1,0:T(8,128)} %get-tuple-element.22) | copy-start | bytes 24580
  148.2 4.8 %copy-start.1 = (bf16[2,4,512,128]{3,2,1,0:T(8,128)(2,1)S(1)}, bf16[2,4,512,128]{3,2,1,0:T(8,128)(2,1)}, u32[]{:S(2)}) copy-start(bf16[2,4,512,128]{3,2,1,0:T(8,128)(2,1)} %get-tuple-element.25) | copy-start | bytes 3145732
  153.3 2.4 %copy-start = (bf16[640,1024]{1,0:T(8,128)(2,1)S(1)}, bf16[640,1024]{1,0:T(8,128)(2,1)}, u32[]{:S(2)}) copy-start(bf16[640,1024]{1,0:T(8,128)(2,1)} %get-tuple-element.24) | copy-start | bytes 3932164
  155.7 2.1 %copy-start.3 = (bf16[128,1024]{1,0:T(8,128)(2,1)S(1)}, bf16[128,1024]{1,0:T(8,128)(2,1)}, u32[]{:S(2)}) copy-start(bf16[128,1024]{1,0:T(8,128)(2,1)} %get-tuple-element.87) | copy-start | bytes 786436
  155.7 2.8 %copy-start.2 = (bf16[128,1024]{1,0:T(8,128)(2,1)S(1)}, bf16[128,1024]{1,0:T(8,128)(2,1)}, u32[]{:S(2)}) copy-start(bf16[128,1024]{1,0:T(8,128)(2,1)} %get-tuple-element.88) | copy-start | bytes 786436

commit v2 on v1

v2 whole, which is shorter than its diff:
```python
import functools

import jax
import jax.numpy as jnp
from jax import lax
from jax.experimental import pallas as pl
from jax.experimental.pallas import tpu as pltpu
from jax.sharding import PartitionSpec as P

BF = jnp.bfloat16
F32 = jnp.float32
MESH = pl.DeviceIdType.MESH
SEMS = 176


def flip(value, mask):
    out = value
    bit = 1
    while bit <= mask:
        if mask & bit:
            out = out + bit - 2 * bit * lax.rem(lax.div(value, bit), 2)
        bit *= 2
    return out


def nt(left, right):
    return lax.dot_general(left, right, (((1,), (1,)), ((), ())), preferred_element_type=F32)


def nn(left, right):
    return jnp.dot(left, right, preferred_element_type=F32)


def fold(block):
    return jnp.sum(block.reshape(block.shape[0] // 8, 8, block.shape[1]), axis=0)


def kernel(
    hid_ref, g_ref, seg_ref, gain1_ref, shift1_ref, gain2_ref, shift2_ref, wqkv_ref, bqkv_ref, wdense_ref,
    bdense_ref, wup_ref, bup_ref, wdown_ref, bdown_ref,
    out_ref, ing_ref, f1_ref, o2_ref, o3_ref, v1_ref, v2_ref, v3_ref, v4_ref, vq_ref, vd_ref, vu_ref, vw_ref,
    f2_ref, f3_ref, PKO, SGO, WD, WN,
    HB, GB, SG, PK, WQ, WU, VEC, B24, XH, N1, N2, QKP, TAB, START, QTM, QM, KT, K, V, VT,
    GP, ACT, ACTT, PT, CTXT, CTX, DCM, DCTM, DG, DGT, DQT, DK, DV, M, MT,
    PB, PRA, PRB, PRX, PRZ, PTX, PUB, DB, DRA, DRB, DRX, DRZ, DTX, DUB, ACC,
    G1, X1, C1, R1, S1, G2, X2, C2, R2, S2, A2, G3, X3, C3, R3, S3, A3,
    SUMS, CG, CDG, SV, SVR, LV, LVX, LC, LCR,
    ssem, rsem, lsem,
):
    r = lax.axis_index("rep")
    s = lax.axis_index("shard")
    c = lax.rem(r, 2)
    chip = lax.div(r, 2)
    y = lax.rem(chip, 4)
    z = lax.div(s, 2)
    l = lax.rem(s, 2)
    other = 1 - l
    half = lax.rem(c + s, 2)
    ahead = lax.rem(z + 1, 4)
    behind = lax.rem(z + 3, 4)
    across_z = lax.rem(z + 2, 4)

    def shard_to(k):
        return {"shard": flip(s, k)}

    def chip_to(k):
        return {"rep": flip(chip, k) * 2 + c}

    partner = {"rep": chip * 2 + 1 - c}
    zk = [None] + [flip(z, k) for k in (1, 2, 3)]

    def lanes(start, size):
        return pl.ds(pl.multiple_of(start, 128), size)

    def rows(start, size):
        return pl.ds(pl.multiple_of(start, 16), size)

    barrier = pltpu.get_barrier_semaphore()
    peers = [shard_to(k) for k in range(1, 8)] + [chip_to(k) for k in range(1, 8)] + [partner]
    for peer in peers:
        pl.semaphore_signal(barrier, inc=1, device_id=peer, device_id_type=MESH)

    mine16 = rows(64 * c + 16 * y, 16)
    local = [
        pltpu.make_async_copy(hid_ref, HB.at[z, l], lsem.at[0]),
        pltpu.make_async_copy(g_ref, GB.at[z, l], lsem.at[1]),
        pltpu.make_async_copy(wdense_ref, WD, lsem.at[2]),
        pltpu.make_async_copy(wdown_ref, WN, lsem.at[3]),
        pltpu.make_async_copy(wup_ref.at[mine16, lanes(512 * s, 512)], WU.at[s, mine16], lsem.at[4]),
    ]
    for j in range(3):
        local.append(pltpu.make_async_copy(
            wqkv_ref.at[mine16, lanes(1024 * j + 128 * s, 128)],
            WQ.at[s, mine16, 128 * j : 128 * j + 128], lsem.at[5 + j]))
    for copy in local:
        copy.start()
    PKO[...] = jnp.zeros_like(PKO)
    at = 0
    for ref in (gain1_ref, shift1_ref, gain2_ref, shift2_ref, bqkv_ref, bdense_ref, bup_ref, bdown_ref):
        size = ref.shape[0] // 128
        PKO[at : at + size] = ref[...].astype(F32).reshape(size, 128)
        at += size
    PK[s] = PKO[...]
    SGO[...] = jnp.broadcast_to(seg_ref[...].reshape(1, 128), (8, 128))
    SG[s] = SGO[...]
    for copy in local:
        copy.wait()
    pl.semaphore_wait(barrier, len(peers))

    used = [0]
    sent = []

    def remote(src, dst, device):
        at = used[0]
        used[0] += 1
        copy = pltpu.make_async_remote_copy(
            src_ref=src, dst_ref=dst, send_sem=ssem.at[at], recv_sem=rsem.at[at],
            device_id=device, device_id_type=MESH,
        )
        copy.start()
        sent.append(copy)
        return copy

    def arrived(copies):
        for copy in copies:
            copy.wait_recv()

    up = {"shard": ahead * 2 + l}
    down = {"shard": behind * 2 + l}

    def pass_on(XB, zz, ll, part, device):
        return remote(XB.at[zz, ll, part], XB.at[zz, ll, part], device)

    def gather_start(x_ref, XB):
        first = remote(x_ref.at[0:64], XB.at[z, l, 0:64], shard_to(1))
        za = remote(x_ref, XB.at[z, l], up)
        zb = remote(x_ref, XB.at[z, l], down)
        last = remote(x_ref.at[64:128], XB.at[z, l, 64:128], shard_to(1))
        return XB, first, za, zb, last

    low = slice(0, 64)
    high = slice(64, 128)

    def gather_next(state):
        XB, first, za, zb, last = state
        first.wait_recv()
        xa = pass_on(XB, z, other, low, up)
        xb = pass_on(XB, z, other, low, down)
        za.wait_recv()
        d2a = pass_on(XB, behind, l, low, up)
        fa = pass_on(XB, behind, l, high, shard_to(1))
        zb.wait_recv()
        d2b = pass_on(XB, ahead, l, high, down)
        fb = pass_on(XB, ahead, l, high, shard_to(1))
        return XB, xa, xb, d2a, d2b, [last, fa, fb]

    def gather_last(state):
        XB, xa, xb, d2a, d2b, rest = state
        xa.wait_recv()
        x2a = pass_on(XB, behind, other, slice(0, 32), up)
        xb.wait_recv()
        x2b = pass_on(XB, ahead, other, slice(32, 64), down)
        d2b.wait_recv()
        fc = pass_on(XB, across_z, l, high, shard_to(1))
        return rest + [d2a, x2a, x2b, fc]

    def turn_weights(ref, W, width, blocks):
        copies = []
        for k in range(1, 8):
            for j in range(blocks):
                copies.append(remote(
                    ref.at[mine16, lanes(1024 * j + width * flip(s, k), width)],
                    W.at[s, mine16, width * j : width * j + width], shard_to(k)))
        return copies

    def along_y(W):
        return [remote(W.at[:, mine16], W.at[:, mine16], chip_to(k)) for k in (1, 3, 2)]

    mine64 = rows(64 * c, 64)
    turn_q = turn_weights(wqkv_ref, WQ, 128, 3)
    gather_h = gather_start(hid_ref, HB)
    turn_u = turn_weights(wup_ref, WU, 512, 1)
    small = [remote(PKO, PK.at[s], shard_to(k)) for k in range(1, 8)]
    small += [remote(SGO, SG.at[s], shard_to(k)) for k in range(1, 8)]
    arrived(turn_q)
    y_q = along_y(WQ)
    gather_h = gather_next(gather_h)
    arrived(turn_u)
    y_u = along_y(WU)
    rest_h = gather_last(gather_h)
    arrived(y_q)
    core_q = remote(WQ.at[:, mine64], WQ.at[:, mine64], partner)
    gather_g = gather_start(g_ref, GB)
    arrived(small)

    for sp in range(8):
        block = PK[sp]
        at = slice(128 * sp, 128 * sp + 128)
        for j in range(4):
            VEC[j : j + 1, at] = block[j : j + 1]
        VEC[4:5, at] = block[7:8] + block[12:13]
        B24[3 * sp : 3 * sp + 3] = block[4:7]
    own = PKO[...]
    bias_up = jnp.concatenate([own[8 + j : 9 + j] for j in range(4)], axis=1)
    bias_q = jnp.concatenate([B24[pl.ds(8 * j + s, 1)] for j in range(3)], axis=1)
    seg_row = jnp.concatenate([SG[sp, 0:1] for sp in range(8)], axis=1).astype(F32)
    count = jnp.zeros((1, 1024), F32)
    for sp in range(8):
        column = jnp.transpose(jnp.broadcast_to(SG[sp, 0:1].astype(F32), (128, 128)))[:, 0:1]
        count = count + jnp.sum((column < seg_row).astype(F32), axis=0, keepdims=True)
    START[...] = jnp.broadcast_to(count.astype(jnp.int32), (8, 1024))
    place = lax.broadcasted_iota(jnp.int32, (8, 1024), 1).astype(F32)
    row8 = lax.broadcasted_iota(jnp.int32, (8, 1024), 0)
    inverse = jnp.zeros((8, 1024), F32)
    for j in range(8):
        inverse = jnp.where(row8 == j, 10000.0 ** (-j / 8.0), inverse)
    angles = (place - count) * inverse
    TAB[0] = jnp.cos(angles)
    TAB[1] = jnp.sin(angles)
    arrived(y_u)
    core_u = remote(WU.at[:, mine64], WU.at[:, mine64], partner)
    arrived(rest_h)
    core_q.wait_recv()

    gain1, shift1, gain2, shift2 = (VEC[j : j + 1] for j in range(4))

    @pl.loop(0, 4)
    def _(i):
        at = rows(256 * i, 256)
        cols = lanes(256 * i, 256)
        block = HB[i].reshape(256, 1024).astype(F32)
        center = block - jnp.mean(block, axis=-1, keepdims=True)
        spread = jnp.mean(center * center, axis=-1, keepdims=True)
        xhat = center * lax.rsqrt(spread + 1e-05)
        XH[at] = xhat.astype(BF)
        n1 = (xhat * gain1 + shift1).astype(BF)
        N1[at] = n1
        N2[at] = (xhat * gain2 + shift2).astype(BF)
        mixed = nn(n1, WQ[...].reshape(1024, 384)) + bias_q
        QKP[:, cols] = jnp.transpose(mixed[:, :256])
        V[at] = mixed[:, 256:].astype(BF)
        VT[:, cols] = jnp.transpose(mixed[:, 256:]).astype(BF)

    gather_g = gather_next(gather_g)

    cosine = TAB[0]
    sine = TAB[1]
    for base in (0, 64, 128, 192):
        one = QKP[base : base + 8]
        two = QKP[base + 8 : base + 16]
        QKP[base : base + 8] = one * cosine - two * sine
        QKP[base + 8 : base + 16] = two * cosine + one * sine
    queries = QKP[0:128].astype(BF).astype(F32) * 0.125
    keys = QKP[128:256]
    low_rows = lax.broadcasted_iota(jnp.int32, (128, 1024), 0) < 64
    low_cols = lax.broadcasted_iota(jnp.int32, (1024, 128), 1) < 64
    QTM[0] = jnp.where(low_rows, queries, 0.0).astype(BF)
    QTM[1] = jnp.where(low_rows, 0.0, queries).astype(BF)
    back = jnp.transpose(queries)
    QM[0] = jnp.where(low_cols, back, 0.0).astype(BF)
    QM[1] = jnp.where(low_cols, 0.0, back).astype(BF)
    KT[...] = keys.astype(BF)
    K[...] = jnp.transpose(keys).astype(BF)

    @pl.loop(0, 2)
    def _(head):
        hr = rows(64 * head, 64)
        for j in range(4):
            top = 256 * (j + 1)
            q = slice(256 * j, 256 * j + 256)
            scores = nn(K[0:top], QTM[head, :, q])
            ki = lax.broadcasted_iota(jnp.int32, (top, 256), 0)
            qi = lax.broadcasted_iota(jnp.int32, (top, 256), 1) + 256 * j
            allowed = (ki <= qi) & (ki >= START[0:1, q])
            scores = jnp.where(allowed, scores, -1e9)
            weight = jnp.exp(scores - jnp.max(scores, axis=0, keepdims=True))
            probs = (weight * (1.0 / jnp.sum(weight, axis=0, keepdims=True))).astype(BF)
            PT[head, 0:top, q] = probs
            CTXT[hr, q] = nn(VT[hr, 0:top], probs).astype(BF)

    def scatter_start(TB, RA, RB):
        a = [remote(TB.at[zk[k], :, 0:64], RA.at[k - 1], shard_to(2 * k)) for k in (1, 3, 2)]
        b = remote(TB.at[:, other, 64:128], RB, shard_to(1))
        return a, b

    def scatter_middle(state, TB, RA, RB, RX, RZ, TX, UB):
        a, b = state
        arrived(a)
        TX[...] = (
            TB[z, other, 0:64].astype(F32) + RA[0, other].astype(F32)
            + RA[1, other].astype(F32) + RA[2, other].astype(F32)
        ).astype(BF)
        out = [remote(TX, RX, shard_to(1))]
        b.wait_recv()
        for k in (1, 3, 2):
            UB[k - 1] = (TB[zk[k], l, 64:128].astype(F32) + RB[zk[k]].astype(F32)).astype(BF)
            out.append(remote(UB.at[k - 1], RZ.at[k - 1], shard_to(2 * k)))
        return out

    def scatter_end(out, TB, RA, RB, RX, RZ):
        arrived(out)
        ACC[0:64] = (
            TB[z, l, 0:64].astype(F32) + RA[0, l].astype(F32) + RA[1, l].astype(F32)
            + RA[2, l].astype(F32) + RX[...].astype(F32)
        )
        ACC[64:128] = (
            TB[z, l, 64:128].astype(F32) + RB[z].astype(F32) + RZ[0].astype(F32)
            + RZ[1].astype(F32) + RZ[2].astype(F32)
        )

    CTX[...] = jnp.transpose(CTXT[...].astype(F32)).astype(BF)
    rest_g = gather_last(gather_g)
    core_u.wait_recv()

    @pl.loop(0, 4)
    def _(i):
        at = rows(256 * i, 256)
        cols = lanes(256 * i, 256)
        gate = nn(N2[at], WU[...].reshape(1024, 512)) + bias_up
        phi = 0.5 + 0.5 * lax.erf(gate * 0.7071067811865476)
        GP[at] = phi + gate * jnp.exp(-0.5 * gate * gate) * 0.3989422804014327
        active = gate * phi
        rounded = active.astype(BF)
        ACT[at] = rounded
        ACTT[:, cols] = jnp.transpose(active).astype(BF)
        total = nn(CTX[at], WD[...]) + nn(rounded, WN[...])
        PB[i] = total.astype(BF).reshape(2, 128, 1024)

    out_state = scatter_start(PB, PRA, PRB)
    arrived(rest_g)

    low_256 = lax.broadcasted_iota(jnp.int32, (256, 128), 1) < 64
    low_t256 = lax.broadcasted_iota(jnp.int32, (128, 256), 0) < 64

    @pl.loop(0, 4)
    def _(i):
        at = rows(256 * i, 256)
        cols = lanes(256 * i, 256)
        grad = nt(GB[i].reshape(256, 1024), WD[...])
        DCM[0, at] = jnp.where(low_256, grad, 0.0).astype(BF)
        DCM[1, at] = jnp.where(low_256, 0.0, grad).astype(BF)
        turned = jnp.transpose(grad)
        DCTM[0, :, cols] = jnp.where(low_t256, turned, 0.0).astype(BF)
        DCTM[1, :, cols] = jnp.where(low_t256, 0.0, turned).astype(BF)

    DK[...] = jnp.zeros_like(DK)
    DV[...] = jnp.zeros_like(DV)

    @pl.loop(0, 2)
    def _(head):
        hr = rows(64 * head, 64)
        for j in range(4):
            top = 256 * (j + 1)
            q = slice(256 * j, 256 * j + 256)
            probs = PT[head, 0:top, q]
            soft = probs.astype(F32)
            probs_grad = nn(V[0:top], DCTM[head, :, q])
            middle = jnp.sum(soft * probs_grad, axis=0, keepdims=True)
            score_grad = (soft * (probs_grad - middle)).astype(BF)
            DQT[hr, q] = nn(KT[hr, 0:top], score_grad) * 0.125
            DK[0:top] += nn(score_grad, QM[head, q])
            DV[0:top] += nn(probs, DCM[head, q])

    QKP[0:128] = DQT[...]
    QKP[128:256] = jnp.transpose(DK[...])
    for base in (0, 64, 128, 192):
        one = QKP[base : base + 8]
        two = QKP[base + 8 : base + 16]
        QKP[base : base + 8] = one * cosine + two * sine
        QKP[base + 8 : base + 16] = two * cosine - one * sine
    MT[0:256] = QKP[...].astype(BF)
    MT[256:384] = jnp.transpose(DV[...]).astype(BF)

    mine = half

    def pair_start(GR, X):
        return remote(GR.at[:, lanes(512 * (1 - mine), 512)], X, partner)

    def spread_start(pair, GR, X, C, R, size):
        pair.wait_recv()
        C[...] = (GR[:, lanes(512 * mine, 512)].astype(F32) + X[...].astype(F32)).astype(BF)
        return [
            remote(C.at[rows(size * flip(chip, k), size)], R.at[k - 1], chip_to(k)) for k in range(1, 8)
        ]

    def spread_sum(copies, C, R, S, size):
        arrived(copies)
        total = C[rows(size * chip, size)].astype(F32)
        for k in range(7):
            total = total + R[k].astype(F32)
        S[...] = total.astype(BF)

    G3[...] = nn(MT[...], N1[...]).astype(BF)
    pair3 = pair_start(G3, X3)
    M[:, 0:256] = jnp.transpose(QKP[...]).astype(BF)
    M[:, 256:384] = DV[...].astype(BF)

    CG[...] = jnp.zeros_like(CG)
    CDG[...] = jnp.zeros_like(CDG)

    @pl.loop(0, 4)
    def _(i):
        at = rows(256 * i, 256)
        cols = lanes(256 * i, 256)
        block = GB[i].reshape(256, 1024)
        CG[...] += fold(block.astype(F32))
        gate_grad = (nt(block, WN[...]) * GP[at]).astype(BF)
        DG[at] = gate_grad
        wide = gate_grad.astype(F32)
        CDG[...] += fold(wide)
        DGT[:, cols] = jnp.transpose(wide).astype(BF)

    spread3 = spread_start(pair3, G3, X3, C3, R3, 48)
    G2[...] = nn(DGT[...], N2[...]).astype(BF)
    pair2 = pair_start(G2, X2)
    grads = GB[...].reshape(1024, 1024)
    G1[0:512] = nn(ACTT[...], grads).astype(BF)
    G1[512:640] = nn(CTXT[...], grads).astype(BF)
    pair1 = pair_start(G1, X1)
    out_rest = scatter_middle(out_state, PB, PRA, PRB, PRX, PRZ, PTX, PUB)
    spread2 = spread_start(pair2, G2, X2, C2, R2, 64)

    SUMS[...] = jnp.zeros_like(SUMS)

    @pl.loop(0, 4)
    def _(i):
        at = rows(256 * i, 256)
        xhat = XH[at].astype(F32)
        one = nt(M[at], WQ[...].reshape(1024, 384))
        two = nt(DG[at], WU[...].reshape(1024, 512))
        DB[i] = (one * gain1 + two * gain2).astype(BF).reshape(2, 128, 1024)
        SUMS[0] += fold(one * xhat)
        SUMS[1] += fold(one)
        SUMS[2] += fold(two * xhat)
        SUMS[3] += fold(two)

    in_state = scatter_start(DB, DRA, DRB)
    spread1 = spread_start(pair1, G1, X1, C1, R1, 80)

    def give(S, out, size):
        at = rows(size * chip, size)
        out[at, lanes(512 * mine, 512)] = S[...]
        return [
            remote(S, out.at[at, lanes(512 * mine, 512)], chip_to(k)) for k in range(1, 8)
        ]

    source = lax.rem(lax.div(s, 4) + c, 2)
    def turn(S, A, size):
        base = used[0]
        used[0] += 4
        slot = lax.div(s, 2)

        def descriptor(m, device):
            return pltpu.make_async_remote_copy(
                src_ref=S.at[:, 128 * m : 128 * m + 128], dst_ref=A.at[slot],
                send_sem=ssem.at[base + m], recv_sem=rsem.at[base + slot],
                device_id={"shard": device}, device_id_type=MESH,
            )

        for m in range(4):
            device = 4 * half + m

            @pl.when(device != s)
            def _():
                descriptor(m, device).start()

            @pl.when(device == s)
            def _():
                A[slot] = S[:, 128 * m : 128 * m + 128]

        return base

    def turned(base, S, A, size):
        for m in range(4):
            @pl.when(4 * half + m != s)
            def _():
                pltpu.make_async_remote_copy(
                    src_ref=S.at[:, 128 * m : 128 * m + 128], dst_ref=A.at[m],
                    send_sem=ssem.at[base + m], recv_sem=rsem.at[base + m],
                    device_id={"shard": flip(s, 1)}, device_id_type=MESH,
                ).wait_send()

            @pl.when(2 * m + source != s)
            def _():
                pltpu.make_async_remote_copy(
                    src_ref=S.at[:, 128 * m : 128 * m + 128], dst_ref=A.at[m],
                    send_sem=ssem.at[base + m], recv_sem=rsem.at[base + m],
                    device_id={"shard": flip(s, 1)}, device_id_type=MESH,
                ).wait_recv()

    def give_turned(A, out, size):
        at = rows(size * chip, size)
        out[source, :, at] = A[...]
        return [remote(A, out.at[source, :, at], chip_to(k)) for k in range(1, 8)]

    spread_sum(spread3, C3, R3, S3, 48)
    turn3 = turn(S3, A3, 48)

    SV[...] = jnp.zeros_like(SV)
    bias_grad = jnp.sum(fold(M[...].astype(F32)), axis=0, keepdims=True)
    B24[...] = jnp.zeros_like(B24)
    for j in range(3):
        B24[pl.ds(8 * j + s, 1)] = bias_grad[:, 128 * j : 128 * j + 128]
    for sp in range(8):
        at = slice(128 * sp, 128 * sp + 128)
        for j in range(4):
            SV[sp, j : j + 1] = jnp.sum(SUMS[j, :, at], axis=0, keepdims=True)
        SV[sp, 4:7] = B24[3 * sp : 3 * sp + 3]
    vectors = [remote(SV.at[flip(s, k)], SVR.at[k - 1], shard_to(k)) for k in range(1, 8)]

    scatter_end(out_rest, PB, PRA, PRB, PRX, PRZ)
    out_ref[...] = (HB[z, l].astype(F32) + ACC[...] + VEC[4:5]).astype(BF)
    turned(turn3, S3, A3, 48)
    give3 = give_turned(A3, f3_ref, 48)
    spread_sum(spread2, C2, R2, S2, 64)
    turn2 = turn(S2, A2, 64)
    spread_sum(spread1, C1, R1, S1, 80)
    give1 = give(S1, f1_ref, 80)

    arrived(vectors)
    LV[...] = jnp.zeros_like(LV)
    total = SV[s]
    for k in range(7):
        total = total + SVR[k]
    LV[0:7] = total[0:7]
    up_grad = jnp.sum(CDG[...], axis=0, keepdims=True)
    for j in range(4):
        LV[8 + j : 9 + j] = up_grad[:, 128 * j : 128 * j + 128]
    LV[12:13] = jnp.sum(CG[:, lanes(128 * s, 128)], axis=0, keepdims=True)
    pair_v = remote(LV, LVX, partner)

    in_rest = scatter_middle(in_state, DB, DRA, DRB, DRX, DRZ, DTX, DUB)
    turned(turn2, S2, A2, 64)
    give2 = give_turned(A2, f2_ref, 64)
    pair_v.wait_recv()
    LC[...] = LV[...] + LVX[...]
    LCR[chip] = LC[...]
    spread_v = [remote(LC, LCR.at[chip], chip_to(k)) for k in range(1, 8)]

    def flat(F, p, i, out, size):
        block = F[p, i].astype(F32)
        for j in range(size // 128):
            out_at = 128 * (2 * i + p) + 1024 * j if size == 384 else 512 * (2 * i + p) + 128 * j
            piece = jnp.transpose(block[128 * j : 128 * j + 128]).astype(BF)
            out[:, lanes(out_at, 128)] = piece

    arrived(give3)
    last3 = remote(f3_ref.at[source], f3_ref.at[source], partner)
    for i in range(4):
        flat(f3_ref, source, i, o3_ref, 384)
    arrived(give1)
    last1 = remote(f1_ref.at[:, lanes(512 * mine, 512)], f1_ref.at[:, lanes(512 * mine, 512)], partner)
    last3.wait_recv()
    for i in range(4):
        flat(f3_ref, 1 - source, i, o3_ref, 384)
    arrived(give2)
    last2 = remote(f2_ref.at[source], f2_ref.at[source], partner)
    for i in range(4):
        flat(f2_ref, source, i, o2_ref, 512)

    arrived(spread_v)
    total = LCR[0]
    for k in range(1, 8):
        total = total + LCR[k]
    v1_ref[...] = total[0:1].reshape(128)
    v2_ref[...] = total[1:2].reshape(128)
    v3_ref[...] = total[2:3].reshape(128)
    v4_ref[...] = total[3:4].reshape(128)
    vq_ref[...] = total[4:7].reshape(384)
    vu_ref[...] = total[8:12].reshape(512)
    vd_ref[...] = total[12:13].reshape(128)
    vw_ref[...] = total[12:13].reshape(128)
    last2.wait_recv()
    for i in range(4):
        flat(f2_ref, 1 - source, i, o2_ref, 512)

    scatter_end(in_rest, DB, DRA, DRB, DRX, DRZ)
    block = HB[z, l].astype(F32)
    center = block - jnp.mean(block, axis=-1, keepdims=True)
    spread = jnp.mean(center * center, axis=-1, keepdims=True)
    scale = lax.rsqrt(spread + 1e-05)
    xhat = center * scale
    grad = ACC[...]
    grad = grad - jnp.mean(grad, axis=-1, keepdims=True) - xhat * jnp.mean(grad * xhat, axis=-1, keepdims=True)
    ing_ref[...] = (GB[z, l].astype(F32) + scale * grad).astype(BF)

    last1.wait_recv()
    for copy in sent:
        copy.wait_send()
    assert used[0] <= SEMS, used[0]


def block_call(*args):
    vm = pltpu.VMEM
    scratch = [
        vm((2, 4, 512, 128), BF), vm((2, 4, 384, 128), BF), vm((16, 128), F32), vm((8, 128), jnp.int32),
        vm((128, 1024), BF), vm((512, 1024), BF),
        vm((4, 2, 128, 1024), BF), vm((4, 2, 128, 1024), BF), vm((8, 8, 128), jnp.int32), vm((8, 16, 128), F32),
        vm((8, 128, 384), BF), vm((8, 128, 512), BF), vm((8, 1024), F32), vm((24, 128), F32),
        vm((1024, 1024), BF), vm((1024, 1024), BF), vm((1024, 1024), BF), vm((256, 1024), F32),
        vm((2, 8, 1024), F32), vm((8, 1024), jnp.int32),
        vm((2, 128, 1024), BF), vm((2, 1024, 128), BF), vm((128, 1024), BF), vm((1024, 128), BF),
        vm((1024, 128), BF), vm((128, 1024), BF),
        vm((1024, 512), F32), vm((1024, 512), BF), vm((512, 1024), BF), vm((2, 1024, 1024), BF),
        vm((128, 1024), BF), vm((1024, 128), BF), vm((2, 1024, 128), BF), vm((2, 128, 1024), BF),
        vm((1024, 512), BF), vm((512, 1024), BF), vm((128, 1024), F32), vm((1024, 128), F32), vm((1024, 128), F32),
        vm((1024, 384), BF), vm((384, 1024), BF),
    ]
    for _ in range(2):
        scratch += [
            vm((4, 2, 128, 1024), BF), vm((3, 2, 64, 1024), BF), vm((4, 64, 1024), BF), vm((64, 1024), BF),
            vm((3, 64, 1024), BF), vm((64, 1024), BF), vm((3, 64, 1024), BF),
        ]
    scratch += [vm((128, 1024), F32)]
    scratch += [vm((640, 1024), BF), vm((640, 512), BF), vm((640, 512), BF), vm((7, 80, 512), BF), vm((80, 512), BF)]
    for size in (64, 48):
        scratch += [
            vm((8 * size, 1024), BF), vm((8 * size, 512), BF), vm((8 * size, 512), BF), vm((7, size, 512), BF),
            vm((size, 512), BF), vm((4, size, 128), BF),
        ]
    scratch += [
        vm((4, 8, 1024), F32), vm((8, 1024), F32), vm((8, 512), F32), vm((8, 16, 128), F32), vm((7, 16, 128), F32),
        vm((16, 128), F32), vm((16, 128), F32), vm((16, 128), F32), vm((8, 16, 128), F32),
        pltpu.SemaphoreType.DMA((SEMS,)), pltpu.SemaphoreType.DMA((SEMS,)), pltpu.SemaphoreType.DMA((8,)),
    ]
    return pl.pallas_call(
        kernel,
        out_shape=(
            jax.ShapeDtypeStruct((128, 1024), BF), jax.ShapeDtypeStruct((128, 1024), BF),
            jax.ShapeDtypeStruct((640, 1024), BF), jax.ShapeDtypeStruct((128, 4096), BF),
            jax.ShapeDtypeStruct((128, 3072), BF),
        ) + tuple(jax.ShapeDtypeStruct((size,), F32) for size in (128, 128, 128, 128, 384, 128, 512, 128)),
        in_specs=[
            pl.BlockSpec(memory_space=pl.ANY if len(arg.shape) == 2 else pltpu.VMEM) for arg in args
        ],
        out_specs=[pl.BlockSpec(memory_space=pltpu.VMEM)] * 13,
        scratch_shapes=scratch,
        compiler_params=pltpu.CompilerParams(
            collective_id=0, has_side_effects=True, vmem_limit_bytes=62 * 2**20
        ),
    )(*args)


def shards(*args):
    out, ing, first, up, qkv, v1, v2, v3, v4, vq, vd, vu, vw = block_call(*args)
    first = first.astype(F32)
    return (
        out, ing, v1, v2, v3, v4, qkv.astype(F32), vq, first[512:640], vd, up.astype(F32), vu, first[0:512], vw,
    )


def solution(mesh):
    both, one, wide = P(("rep", "shard"), None), P("shard"), P("shard", None)
    placed = (
        both, both, P(("rep", "shard")), one, one, one, one, wide, one, wide, one, wide, one, wide, one,
    )
    return jax.shard_map(
        shards, mesh=mesh, in_specs=placed,
        out_specs=(both, both, one, one, one, one, wide, one, wide, one, wide, one, wide, one),
        check_vma=False,
    )
```

time: 162 us -> 133 us (0.82); the launches traced: 159 us -> 133 us
  Pallas kernels: 135 us -> 119 us
  local copies, waits for them, and re-layouts: 22.1 us -> 10.4 us
    pallas_call x1, Pallas kernels: 135 us -> 119 us  [block_call(): pl.pallas_call(kernel, out_shape=(jax.ShapeDtypeStruct((128, 1024), BF),...]
    unnamed x26 -> x34, local copies, waits for them, and re-layouts: 11 us -> 5.68 us
    reshape x5 -> x0, local copies, waits for them, and re-layouts: 4.88 us -> none  [the longest x2 3.57 us: shards(): grad_qkv = jnp.transpose(third, (4, 2, 1, 0, 3)).reshape(128, 3072)]
    convert_element_type x0 -> x2, other arithmetic: none -> 2.82 us  [the longest x1 1.53 us: shards(): up.astype(F32)]
where the time goes in v2:
time: 133 us
  Pallas kernels  119 us (89%)
  local copies, waits for them, and re-layouts  10.4 us (8%)
  other arithmetic  2.82 us (2%)
    pallas_call x1, Pallas kernels, block_call(): pl.pallas_call(kernel, out_shape=(jax.ShapeDtypeStruct((128, 1024), BF),...  119 us
    unnamed x34, local copies, waits for them, and re-layouts  5.68 us
    slice x1, local copies, waits for them, and re-layouts, shards(): first[0:512]  2.88 us

profile of v2, /device:TPU:1, one launch (start us, length us, event | category | flops | bytes accessed | tf_op | source)
XLA Modules:
  0.0 133.2 jit_solution(248986060942531852)
XLA Ops:
  0.7 119.2 %shard_map.254 = (bf16[128,1024]{1,0:T(8,128)(2,1)}, bf16[128,1024]{1,0:T(8,128)(2,1)}, bf16[640,1024]{1,0:T(8,128)(2,1)}, bf16[128,4096]{1,0:T(8,128)(2,1)}, bf...) custom-call(bf16[128,1024]{1,0:T(8,128)(2,1)} %hid_ref.1, ...), custom_call_target="tpu_custom_call" | custom-call | tf_op jit(solution)/shard_map/pallas_call | solution.py:626
  119.9 0.0 copy-start
  119.9 2.9 %slice.9 = f32[512,1024]{1,0:T(8,128)} slice(bf16[640,1024]{1,0:T(8,128)(2,1)} %get-tuple-element.35), slice={[0:512], [0:1024]} | slice | bytes 4194304 | tf_op jit(solution)/shard_map/slice | solution.py:648
  122.8 1.9 %slice.8 = f32[128,1024]{1,0:T(8,128)} slice(bf16[640,1024]{1,0:T(8,128)(2,1)} %get-tuple-element.35), slice={[512:640], [0:1024]} | slice | bytes 1048576 | tf_op jit(solution)/shard_map/slice | solution.py:648
  124.7 0.0 copy-done
  124.7 1.5 %convert_element_type.11 = f32[128,4096]{1,0:T(8,128)} convert(bf16[128,4096]{1,0:T(8,128)(2,1)S(1)} %copy-done) | non-fusion elementwise | flops 524288 | bytes 3145728 | tf_op jit(solution)/shard_map/convert_element_type | solution.py:648
  126.2 0.0 copy-start.8
  126.2 0.0 copy-start.5
  126.2 0.0 copy-start.7
  126.2 0.0 copy-start.4
  126.2 0.0 copy-start.6
  126.3 0.0 copy-done.1
  126.3 1.3 convert_element_type.9
  127.6 0.0 copy-done.3
  127.6 0.7 copy.39
  128.3 0.0 copy-done.2
  128.3 0.7 copy.40
  129.0 0.0 copy-done.11
  129.0 0.5 copy.41
  129.5 0.0 copy-done.10
  129.5 0.5 copy.42
  130.0 0.0 copy-done.9
  130.0 0.5 copy.43
  130.5 0.0 copy-done.8
  130.5 0.5 copy.44
  131.0 0.0 copy-done.5
  131.0 0.6 copy.45
  131.6 0.0 copy-done.7
  131.6 0.5 copy.46
  132.1 0.0 copy-done.4
  132.1 0.6 copy.47
  132.7 0.5 copy.48
  (7 shorter events, 0.0 us)
Async XLA Ops:
  119.9 4.8 %copy-start = (bf16[128,4096]{1,0:T(8,128)(2,1)S(1)}, bf16[128,4096]{1,0:T(8,128)(2,1)}, u32[]{:S(2)}) copy-start(bf16[128,4096]{1,0:T(8,128)(2,1)} %get-tuple-element.37) | copy-start | bytes 3145732
  122.8 3.5 %copy-start.1 = (bf16[128,3072]{1,0:T(8,128)(2,1)S(1)}, bf16[128,3072]{1,0:T(8,128)(2,1)}, u32[]{:S(2)}) copy-start(bf16[128,3072]{1,0:T(8,128)(2,1)} %get-tuple-element.33) | copy-start | bytes 2359300
  124.7 2.9 %copy-start.3 = (bf16[128,1024]{1,0:T(8,128)(2,1)S(1)}, bf16[128,1024]{1,0:T(8,128)(2,1)}, u32[]{:S(2)}) copy-start(bf16[128,1024]{1,0:T(8,128)(2,1)} %get-tuple-element.54) | copy-start | bytes 786436
  126.2 2.1 %copy-start.2 = (bf16[128,1024]{1,0:T(8,128)(2,1)S(1)}, bf16[128,1024]{1,0:T(8,128)(2,1)}, u32[]{:S(2)}) copy-start(bf16[128,1024]{1,0:T(8,128)(2,1)} %get-tuple-element.55) | copy-start | bytes 786436
  126.2 2.8 %copy-start.11 = (f32[128]{0:T(128)S(1)}, f32[128]{0:T(128)}, u32[]{:S(2)}) copy-start(f32[128]{0:T(128)} %get-tuple-element.56) | copy-start | bytes 1540
  126.2 3.3 %copy-start.10 = (f32[128]{0:T(128)S(1)}, f32[128]{0:T(128)}, u32[]{:S(2)}) copy-start(f32[128]{0:T(128)} %get-tuple-element.57) | copy-start | bytes 1540
  126.2 3.8 %copy-start.9 = (f32[128]{0:T(128)S(1)}, f32[128]{0:T(128)}, u32[]{:S(2)}) copy-start(f32[128]{0:T(128)} %get-tuple-element.58) | copy-start | bytes 1540
  126.2 4.3 %copy-start.8 = (f32[128]{0:T(128)S(1)}, f32[128]{0:T(128)}, u32[]{:S(2)}) copy-start(f32[128]{0:T(128)} %get-tuple-element.59) | copy-start | bytes 1540
  126.2 4.8 %copy-start.5 = (f32[384]{0:T(512)S(1)}, f32[384]{0:T(512)}, u32[]{:S(2)}) copy-start(f32[384]{0:T(512)} %get-tuple-element.61) | copy-start | bytes 4612
  126.2 5.4 %copy-start.7 = (f32[128]{0:T(128)S(1)}, f32[128]{0:T(128)}, u32[]{:S(2)}) copy-start(f32[128]{0:T(128)} %get-tuple-element.63) | copy-start | bytes 1540
  126.2 5.9 %copy-start.4 = (f32[512]{0:T(512)S(1)}, f32[512]{0:T(512)}, u32[]{:S(2)}) copy-start(f32[512]{0:T(512)} %get-tuple-element.65) | copy-start | bytes 6148
  126.2 6.5 %copy-start.6 = (f32[128]{0:T(128)S(1)}, f32[128]{0:T(128)}, u32[]{:S(2)}) copy-start(f32[128]{0:T(128)} %get-tuple-element.67) | copy-start | bytes 1540

commit v3 on v2

v3 whole, which is shorter than its diff:
```python
import functools

import jax
import jax.numpy as jnp
from jax import lax
from jax.experimental import pallas as pl
from jax.experimental.pallas import tpu as pltpu
from jax.sharding import PartitionSpec as P

BF = jnp.bfloat16
F32 = jnp.float32
MESH = pl.DeviceIdType.MESH
SEMS = 176


def flip(value, mask):
    out = value
    bit = 1
    while bit <= mask:
        if mask & bit:
            out = out + bit - 2 * bit * lax.rem(lax.div(value, bit), 2)
        bit *= 2
    return out


def nt(left, right):
    return lax.dot_general(left, right, (((1,), (1,)), ((), ())), preferred_element_type=F32)


def nn(left, right):
    return jnp.dot(left, right, preferred_element_type=F32)


def fold(block):
    return jnp.sum(block.reshape(block.shape[0] // 8, 8, block.shape[1]), axis=0)


def kernel(
    hid_ref, g_ref, seg_ref, gain1_ref, shift1_ref, gain2_ref, shift2_ref, wqkv_ref, bqkv_ref, wdense_ref,
    bdense_ref, wup_ref, bup_ref, wdown_ref, bdown_ref,
    out_ref, ing_ref, dn_ref, de_ref, o2_ref, o3_ref, v1_ref, v2_ref, v3_ref, v4_ref, vq_ref, vd_ref, vu_ref, vw_ref,
    f1_ref, f2_ref, f3_ref, PKO, SGO, SGX, WD, WN, OWNH, OWNG,
    HB, GB, SG, PK, WQ, WU, VEC, B24, XH, N1, N2, QKP, TAB, START, QTM, QM, KT, K, V, VT,
    GP, ACT, ACTT, PT, CTXT, CTX, DCM, DCTM, DG, DGT, DQT, DK, DV, M, MT,
    PB, PRA, PRT, PRZ, PFX, PRX, DB, DRA, DRT, DRZ, DFX, DRX, ACC,
    G1, X1, C1, R1, S1, CY1, RH1, G2, X2, C2, R2, S2, CY2, RH2, A2, G3, X3, C3, R3, S3, A3,
    SUMS, CG, CDG, SV, SVR, LV, LVX, LC, LCR,
    ssem, rsem, lsem,
):
    r = lax.axis_index("rep")
    s = lax.axis_index("shard")
    k = lax.rem(r, 2)
    chip = lax.div(r, 2)
    y = lax.rem(chip, 4)
    h = lax.div(chip, 4)
    z = lax.div(s, 2)
    l = lax.rem(s, 2)
    b = 2 * z + k
    home = k == l
    off = k != l
    zs = (lax.rem(z + 2, 4), lax.rem(z + 1, 4), lax.rem(z + 3, 4))
    across_z, ahead, behind = zs

    def shard_to(m):
        return {"shard": flip(s, m)}

    def chip_to(m):
        return {"rep": flip(chip, m) * 2 + k}

    def z_to(zz):
        return {"shard": 2 * zz + l}

    partner = {"rep": chip * 2 + 1 - k}
    x_near = {"shard": 2 * z + 1 - l}
    x_far = {"rep": (1 - h) * 8 + y * 2 + k, "shard": 2 * z + 1 - l}
    x_cross = {"rep": chip * 2 + 1 - k, "shard": 2 * z + 1 - l}

    def lanes(start, size):
        return pl.ds(pl.multiple_of(start, 128), size)

    def rows(start, size):
        return pl.ds(pl.multiple_of(start, 16), size)

    barrier = pltpu.get_barrier_semaphore()
    peers = [shard_to(m) for m in range(1, 8)] + [chip_to(m) for m in range(1, 8)] + [partner, x_far, x_cross]
    for peer in peers:
        pl.semaphore_signal(barrier, inc=1, device_id=peer, device_id_type=MESH)

    local = [
        pltpu.make_async_copy(hid_ref, OWNH, lsem.at[0]),
        pltpu.make_async_copy(g_ref, OWNG, lsem.at[1]),
        pltpu.make_async_copy(
            wup_ref.at[rows(32 * y, 32), lanes(512 * b, 512)], WU.at[z, l, rows(32 * y, 32)], lsem.at[2]),
    ]
    for j in range(3):
        local.append(pltpu.make_async_copy(
            wqkv_ref.at[:, lanes(1024 * j + 128 * b, 128)], WQ.at[z, l, :, 128 * j : 128 * j + 128], lsem.at[3 + j]))
    own_only = [
        pltpu.make_async_copy(hid_ref, HB.at[z, k], lsem.at[6]),
        pltpu.make_async_copy(g_ref, GB.at[z, k], lsem.at[7]),
        pltpu.make_async_copy(wdense_ref, WD, lsem.at[8]),
        pltpu.make_async_copy(wdown_ref, WN, lsem.at[9]),
    ]
    for copy in local:
        copy.start()

    @pl.when(home)
    def _():
        for copy in own_only:
            copy.start()

    PKO[...] = jnp.zeros_like(PKO)
    at = 0
    for ref in (gain1_ref, shift1_ref, gain2_ref, shift2_ref, bqkv_ref, bdense_ref, bup_ref, bdown_ref):
        size = ref.shape[0] // 128
        PKO[at : at + size] = ref[...].astype(F32).reshape(size, 128)
        at += size
    PK[s] = PKO[...]
    SGO[...] = jnp.broadcast_to(seg_ref[...].reshape(1, 128), (8, 128))
    SG[s] = SGO[...]
    for copy in local:
        copy.wait()

    @pl.when(home)
    def _():
        for copy in own_only:
            copy.wait()

    pl.semaphore_wait(barrier, len(peers))

    used = [0]
    sent = []

    class Copy:
        def __init__(self, src, dst, device, send, recv):
            at = used[0]
            used[0] += 1
            self.copy = pltpu.make_async_remote_copy(
                src_ref=src, dst_ref=dst, send_sem=ssem.at[at], recv_sem=rsem.at[at],
                device_id=device, device_id_type=MESH,
            )
            self.send = send
            self.recv = recv
            sent.append(self)
            self.under(send, self.copy.start)

        def under(self, role, action):
            if role is None:
                action()
            else:
                pl.when(role)(lambda: action())

        def wait_recv(self):
            self.under(self.recv, self.copy.wait_recv)

        def wait_send(self):
            self.under(self.send, self.copy.wait_send)

    def remote(src, dst, device, send=None, recv=None):
        return Copy(src, dst, device, send, recv)

    def arrived(copies):
        for copy in copies:
            copy.wait_recv()

    low = slice(0, 64)
    high = slice(64, 128)

    def same(ref, device):
        return remote(ref, ref, device)

    def gather_x(x_ref, XB):
        return remote(x_ref, XB.at[z, l], x_cross, off, off)

    def gather_z(first, XB):
        first.wait_recv()
        own = XB.at[z, k]
        return XB, same(own, z_to(ahead)), same(own, z_to(behind)), [same(own, partner)]

    def gather_next(state):
        XB, za, zb, cores = state
        za.wait_recv()
        d2a = same(XB.at[behind, k, low], z_to(ahead))
        cores.append(same(XB.at[behind, k], partner))
        zb.wait_recv()
        d2b = same(XB.at[ahead, k, high], z_to(behind))
        cores.append(same(XB.at[ahead, k], partner))
        return XB, d2a, d2b, cores

    def gather_last(state):
        XB, d2a, d2b, cores = state
        arrived([d2a, d2b])
        cores.append(same(XB.at[across_z, k], partner))
        return cores

    def weight_z(ref, W, width, blocks):
        return [
            [remote(
                ref.at[:, lanes(1024 * j + width * (2 * zz + k), width)],
                W.at[z, l, :, width * j : width * j + width], z_to(zz)) for j in range(blocks)]
            for zz in (ahead, behind, across_z)
        ]

    def weight_x(W, zz):
        return [same(W.at[zz, l, low], x_near), same(W.at[zz, l, high], x_far)]

    y_peers = [{"rep": (4 * h + flip(y, m)) * 2 + k} for m in (1, 3, 2)]
    near32 = rows(32 * y, 16)
    far32 = rows(32 * y + 16, 16)
    both32 = rows(32 * y, 32)
    both128 = rows(128 * y, 128)
    gather_h = gather_x(hid_ref, HB)
    up_z = [
        remote(wup_ref.at[both32, lanes(512 * (2 * zz + k), 512)], WU.at[z, l, both32], z_to(zz))
        for zz in (ahead, behind, across_z)
    ]
    outer_x = [
        remote(wdown_ref.at[rows(128 * y, 64)], WN.at[rows(128 * y, 64)], x_near, home, off),
        remote(wdown_ref.at[rows(128 * y + 64, 64)], WN.at[rows(128 * y + 64, 64)], x_far, home, off),
        remote(wdense_ref.at[near32], WD.at[near32], x_near, home, off),
        remote(wdense_ref.at[far32], WD.at[far32], x_far, home, off),
    ]
    qkv_z = weight_z(wqkv_ref, WQ, 128, 3)
    qkv_x = weight_x(WQ, z)
    gather_h = gather_z(gather_h, HB)
    small = [remote(PKO, PK.at[s], shard_to(m)) for m in range(1, 8)]
    small += [remote(SGO, SG.at[s], shard_to(m)) for m in range(1, 8)]
    arrived(up_z)
    up_x = [same(WU.at[:, l, near32], x_near), same(WU.at[:, l, far32], x_far)]
    arrived(outer_x)
    outer_y = [
        remote(ref.at[part], ref.at[part], peer, off, off)
        for peer in y_peers for ref, part in ((WN, both128), (WD, both32))
    ]
    for copies, zz in zip(qkv_z, (behind, ahead, across_z)):
        arrived(copies)
        qkv_x += weight_x(WQ, zz)
    arrived(up_x)
    up_y = [same(WU.at[:, :, both32], peer) for peer in y_peers]
    gather_h = gather_next(gather_h)
    gather_g = gather_x(g_ref, GB)
    arrived(small)
    seg_core = remote(SG, SGX, partner)
    rest_h = gather_last(gather_h)
    gather_g = gather_z(gather_g, GB)

    for sp in range(8):
        block = PK[sp]
        at = slice(128 * sp, 128 * sp + 128)
        for j in range(4):
            VEC[j : j + 1, at] = block[j : j + 1]
        VEC[4:5, at] = block[7:8] + block[12:13]
        B24[3 * sp : 3 * sp + 3] = block[4:7]
    own = PK[b]
    bias_up = jnp.concatenate([own[8 + j : 9 + j] for j in range(4)], axis=1)
    bias_q = jnp.concatenate([B24[pl.ds(8 * j + b, 1)] for j in range(3)], axis=1)
    seg_core.wait_recv()
    ids = [jnp.where(home, SG[sp, 0:1], SGX[sp, 0:1]).astype(F32) for sp in range(8)]
    seg_row = jnp.concatenate(ids, axis=1)
    count = jnp.zeros((1, 1024), F32)
    for sp in range(8):
        column = jnp.transpose(jnp.broadcast_to(ids[sp], (128, 128)))[:, 0:1]
        count = count + jnp.sum((column < seg_row).astype(F32), axis=0, keepdims=True)
    START[...] = jnp.broadcast_to(count.astype(jnp.int32), (8, 1024))
    place = lax.broadcasted_iota(jnp.int32, (8, 1024), 1).astype(F32)
    row8 = lax.broadcasted_iota(jnp.int32, (8, 1024), 0)
    inverse = jnp.zeros((8, 1024), F32)
    for j in range(8):
        inverse = jnp.where(row8 == j, 10000.0 ** (-j / 8.0), inverse)
    angles = (place - count) * inverse
    TAB[0] = jnp.cos(angles)
    TAB[1] = jnp.sin(angles)
    gain1, shift1, gain2, shift2 = (VEC[j : j + 1] for j in range(4))

    arrived(rest_h)
    arrived(qkv_x)

    @pl.loop(0, 4)
    def _(i):
        at = rows(256 * i, 256)
        cols = lanes(256 * i, 256)
        block = HB[i].reshape(256, 1024).astype(F32)
        center = block - jnp.mean(block, axis=-1, keepdims=True)
        spread = jnp.mean(center * center, axis=-1, keepdims=True)
        xhat = center * lax.rsqrt(spread + 1e-05)
        XH[at] = xhat.astype(BF)
        n1 = (xhat * gain1 + shift1).astype(BF)
        N1[at] = n1
        N2[at] = (xhat * gain2 + shift2).astype(BF)
        mixed = nn(n1, WQ[...].reshape(1024, 384)) + bias_q
        QKP[:, cols] = jnp.transpose(mixed[:, :256])
        V[at] = mixed[:, 256:].astype(BF)
        VT[:, cols] = jnp.transpose(mixed[:, 256:]).astype(BF)

    cosine = TAB[0]
    sine = TAB[1]
    for base in (0, 64, 128, 192):
        one = QKP[base : base + 8]
        two = QKP[base + 8 : base + 16]
        QKP[base : base + 8] = one * cosine - two * sine
        QKP[base + 8 : base + 16] = two * cosine + one * sine
    queries = QKP[0:128].astype(BF).astype(F32) * 0.125
    keys = QKP[128:256]
    low_rows = lax.broadcasted_iota(jnp.int32, (128, 1024), 0) < 64
    low_cols = lax.broadcasted_iota(jnp.int32, (1024, 128), 1) < 64
    QTM[0] = jnp.where(low_rows, queries, 0.0).astype(BF)
    QTM[1] = jnp.where(low_rows, 0.0, queries).astype(BF)
    back = jnp.transpose(queries)
    QM[0] = jnp.where(low_cols, back, 0.0).astype(BF)
    QM[1] = jnp.where(low_cols, 0.0, back).astype(BF)
    KT[...] = keys.astype(BF)
    K[...] = jnp.transpose(keys).astype(BF)

    def attention(head):
        hr = slice(64 * head, 64 * head + 64)
        for j in range(4):
            top = 256 * (j + 1)
            q = slice(256 * j, 256 * j + 256)
            scores = nn(K[0:top], QTM[head, :, q])
            ki = lax.broadcasted_iota(jnp.int32, (top, 256), 0)
            qi = lax.broadcasted_iota(jnp.int32, (top, 256), 1) + 256 * j
            allowed = (ki <= qi) & (ki >= START[0:1, q])
            scores = jnp.where(allowed, scores, -1e9)
            weight = jnp.exp(scores - jnp.max(scores, axis=0, keepdims=True))
            probs = (weight * (1.0 / jnp.sum(weight, axis=0, keepdims=True))).astype(BF)
            PT[head, 0:top, q] = probs
            CTXT[hr, q] = nn(VT[hr, 0:top], probs).astype(BF)

    attention(0)
    gather_g = gather_next(gather_g)
    attention(1)

    def scatter_core(TB, RA):
        return [remote(TB.at[zz, 1 - k], RA.at[zz], partner) for zz in (across_z, ahead, behind, z)]

    def scatter_z(copies, TB, RA, RT, RZ):
        out = []
        for j, zz in enumerate(zs):
            copies[j].wait_recv()
            RT[j] = (TB[zz, k].astype(F32) + RA[zz].astype(F32)).astype(BF)
            out.append(remote(RT.at[j], RZ.at[j], z_to(zz)))
        copies[3].wait_recv()
        return out

    def scatter_x(copies, TB, RA, RZ, FX, RX):
        arrived(copies)
        total = TB[z, k].astype(F32) + RA[z].astype(F32)
        for j in range(3):
            total = total + RZ[j].astype(F32)
        ACC[...] = total
        FX[...] = total.astype(BF)
        return remote(FX, RX, x_cross, off, off)

    def scatter_end(copy, RX):
        copy.wait_recv()

        @pl.when(off)
        def _():
            ACC[...] = RX[...].astype(F32)

    CTX[...] = jnp.transpose(CTXT[...].astype(F32)).astype(BF)
    rest_g = gather_last(gather_g)
    arrived(up_y)
    arrived(outer_y)

    @pl.loop(0, 4)
    def _(i):
        at = rows(256 * i, 256)
        cols = lanes(256 * i, 256)
        gate = nn(N2[at], WU[...].reshape(1024, 512)) + bias_up
        phi = 0.5 + 0.5 * lax.erf(gate * 0.7071067811865476)
        GP[at] = phi + gate * jnp.exp(-0.5 * gate * gate) * 0.3989422804014327
        active = gate * phi
        rounded = active.astype(BF)
        ACT[at] = rounded
        ACTT[:, cols] = jnp.transpose(active).astype(BF)
        total = nn(CTX[at], WD[...]) + nn(rounded, WN[...])
        PB[i] = total.astype(BF).reshape(2, 128, 1024)

    out_cores = scatter_core(PB, PRA)
    arrived(rest_g)

    def near_start(GR, X, size):
        part = lanes(512 * (1 - l), 512)
        top = slice(0, 4 * size)
        end = slice(4 * size, 8 * size)
        return [remote(GR.at[top, part], X.at[top], x_near), remote(GR.at[end, part], X.at[end], x_far)]

    def spread_start(near, GR, X, C, R, size):
        arrived(near)
        C[...] = (GR[:, lanes(512 * l, 512)].astype(F32) + X[...].astype(F32)).astype(BF)
        return [
            remote(C.at[rows(size * flip(chip, m), size)], R.at[m - 1], chip_to(m)) for m in range(1, 8)
        ]

    def spread_sum(copies, C, R, S, size):
        arrived(copies)
        total = C[rows(size * chip, size)].astype(F32)
        for m in range(7):
            total = total + R[m].astype(F32)
        S[...] = total.astype(BF)

    y_at = [flip(y, m) for m in (1, 3, 2)]
    h_peer = {"rep": (4 * (1 - h) + y) * 2 + k}

    def along_y(C, R, size, role=None):
        return [
            remote(C.at[rows(2 * size * yy, 2 * size)], R.at[m], y_peers[m], role, role) for m, yy in enumerate(y_at)
        ]

    def quarter_sum(copies, C, R, CY, size):
        arrived(copies)
        CY[...] = (
            C[rows(2 * size * y, 2 * size)].astype(F32) + R[0].astype(F32) + R[1].astype(F32) + R[2].astype(F32)
        ).astype(BF)

    def along_h(CY, RH, size, role=None):
        return remote(CY.at[rows(size * (1 - h), size)], RH, h_peer, role, role)

    def turn(S, A):
        A[z] = S[:, lanes(128 * z, 128)]
        return [remote(S.at[:, lanes(128 * zz, 128)], A.at[z], z_to(zz)) for zz in (ahead, behind, across_z)]

    def give(copies, A, out, size):
        arrived(copies)
        at = rows(size * chip, size)
        out[k, :, at] = A[...]
        return [remote(A, out.at[k, :, at], chip_to(m)) for m in range(1, 8)]

    def give_h(copies, A, out, size):
        arrived(copies)
        at = rows(size * (2 * y + h), size)
        out[k, :, at] = A[...]
        return remote(A, out.at[k, :, at], h_peer)

    def give_y(copy, out, size):
        copy.wait_recv()
        ref = out.at[k, :, rows(2 * size * y, 2 * size)]
        return [remote(ref, ref, peer) for peer in y_peers]

    def put(GR, total):
        for sp in range(8):
            at = 512 * (sp % 2) + 128 * (sp // 2)
            GR[:, at : at + 128] = total[:, 128 * sp : 128 * sp + 128].astype(BF)

    grads = GB[...].reshape(1024, 1024)
    G1[0:512] = nn(ACTT[...], grads).astype(BF)
    G1[512:640] = nn(CTXT[...], grads).astype(BF)
    y1 = along_y(G1, R1, 80)

    CG[...] = jnp.zeros_like(CG)
    CDG[...] = jnp.zeros_like(CDG)

    @pl.loop(0, 4)
    def _(i):
        at = rows(256 * i, 256)
        cols = lanes(256 * i, 256)
        block = GB[i].reshape(256, 1024)
        CG[...] += fold(block.astype(F32))
        gate_grad = (nt(block, WN[...]) * GP[at]).astype(BF)
        DG[at] = gate_grad
        wide = gate_grad.astype(F32)
        CDG[...] += fold(wide)
        DGT[:, cols] = jnp.transpose(wide).astype(BF)

    out_z = scatter_z(out_cores, PB, PRA, PRT, PRZ)
    put(G2, nn(DGT[...], N2[...]))
    near2 = near_start(G2, X2, 64)

    low_256 = lax.broadcasted_iota(jnp.int32, (256, 128), 1) < 64
    low_t256 = lax.broadcasted_iota(jnp.int32, (128, 256), 0) < 64

    @pl.loop(0, 4)
    def _(i):
        at = rows(256 * i, 256)
        cols = lanes(256 * i, 256)
        grad = nt(GB[i].reshape(256, 1024), WD[...])
        DCM[0, at] = jnp.where(low_256, grad, 0.0).astype(BF)
        DCM[1, at] = jnp.where(low_256, 0.0, grad).astype(BF)
        turned = jnp.transpose(grad)
        DCTM[0, :, cols] = jnp.where(low_t256, turned, 0.0).astype(BF)
        DCTM[1, :, cols] = jnp.where(low_t256, 0.0, turned).astype(BF)

    DK[...] = jnp.zeros_like(DK)
    DV[...] = jnp.zeros_like(DV)

    def attention_back(head):
        hr = slice(64 * head, 64 * head + 64)
        for j in range(4):
            top = 256 * (j + 1)
            q = slice(256 * j, 256 * j + 256)
            probs = PT[head, 0:top, q]
            soft = probs.astype(F32)
            probs_grad = nn(V[0:top], DCTM[head, :, q])
            middle = jnp.sum(soft * probs_grad, axis=0, keepdims=True)
            score_grad = (soft * (probs_grad - middle)).astype(BF)
            DQT[hr, q] = nn(KT[hr, 0:top], score_grad) * 0.125
            DK[0:top] += nn(score_grad, QM[head, q])
            DV[0:top] += nn(probs, DCM[head, q])

    attention_back(0)
    attention_back(1)
    arrived(near2)
    C2[...] = (G2[:, lanes(512 * l, 512)].astype(F32) + X2[...].astype(F32)).astype(BF)
    y2 = along_y(C2, R2, 64)

    QKP[0:128] = DQT[...]
    QKP[128:256] = jnp.transpose(DK[...])
    for base in (0, 64, 128, 192):
        one = QKP[base : base + 8]
        two = QKP[base + 8 : base + 16]
        QKP[base : base + 8] = one * cosine + two * sine
        QKP[base + 8 : base + 16] = two * cosine - one * sine
    MT[0:256] = QKP[...].astype(BF)
    MT[256:384] = jnp.transpose(DV[...]).astype(BF)

    put(G3, nn(MT[...], N1[...]))
    near3 = near_start(G3, X3, 48)
    M[:, 0:256] = jnp.transpose(QKP[...]).astype(BF)
    M[:, 256:384] = DV[...].astype(BF)
    SUMS[...] = jnp.zeros_like(SUMS)
    in_cores = []
    in_z = []

    def norm_grads(zz):
        at = rows(256 * zz, 256)
        xhat = XH[at].astype(F32)
        one = nt(M[at], WQ[...].reshape(1024, 384))
        two = nt(DG[at], WU[...].reshape(1024, 512))
        DB[zz] = (one * gain1 + two * gain2).astype(BF).reshape(2, 128, 1024)
        in_cores.append(remote(DB.at[zz, 1 - k], DRA.at[zz], partner))
        SUMS[0] += fold(one * xhat)
        SUMS[1] += fold(one)
        SUMS[2] += fold(two * xhat)
        SUMS[3] += fold(two)

    def norm_send(j):
        zz = zs[j]
        in_cores[j].wait_recv()
        DRT[j] = (DB[zz, k].astype(F32) + DRA[zz].astype(F32)).astype(BF)
        in_z.append(remote(DRT.at[j], DRZ.at[j], z_to(zz)))

    norm_grads(across_z)
    norm_grads(ahead)
    norm_send(0)
    quarter_sum(y1, G1, R1, CY1, 80)
    near1 = [
        remote(CY1.at[0:80], X1.at[0:80], x_near, off, home),
        remote(CY1.at[80:160], X1.at[80:160], x_far, off, home),
    ]
    norm_grads(behind)
    norm_send(1)
    norm_grads(z)
    norm_send(2)
    out_x = scatter_x(out_z, PB, PRA, PRZ, PFX, PRX)

    SV[...] = jnp.zeros_like(SV)
    bias_grad = jnp.sum(fold(M[...].astype(F32)), axis=0, keepdims=True)
    B24[...] = jnp.zeros_like(B24)
    for j in range(3):
        B24[pl.ds(8 * j + b, 1)] = bias_grad[:, 128 * j : 128 * j + 128]
    for sp in range(8):
        at = slice(128 * sp, 128 * sp + 128)
        for j in range(4):
            SV[sp, j : j + 1] = jnp.sum(SUMS[j, :, at], axis=0, keepdims=True)
        SV[sp, 4:7] = B24[3 * sp : 3 * sp + 3]
    up_grad = jnp.sum(CDG[...], axis=0, keepdims=True)
    for j in range(4):
        SV[b, 8 + j : 9 + j] = up_grad[:, 128 * j : 128 * j + 128]
    SV[b, 12:13] = jnp.sum(CG[:, lanes(128 * b, 128)], axis=0, keepdims=True)
    vectors = [remote(SV.at[flip(s, m)], SVR.at[m - 1], shard_to(m)) for m in range(1, 8)]

    spread3 = spread_start(near3, G3, X3, C3, R3, 48)
    quarter_sum(y2, C2, R2, CY2, 64)
    h2 = along_h(CY2, RH2, 64)
    arrived(near1)

    @pl.when(home)
    def _():
        C1[...] = (CY1[...].astype(F32) + X1[...].astype(F32)).astype(BF)

    h1 = along_h(C1, RH1, 80, home)
    scatter_end(out_x, PRX)
    out_ref[...] = (OWNH[...].astype(F32) + ACC[...] + VEC[4:5]).astype(BF)
    arrived(vectors)
    total = SV[s]
    for m in range(7):
        total = total + SVR[m]
    LV[...] = total
    pair_v = remote(LV, LVX, partner)
    h1.wait_recv()

    @pl.when(home)
    def _():
        S1[...] = (C1[rows(80 * h, 80)].astype(F32) + RH1[...].astype(F32)).astype(BF)
        f1_ref[y, h] = S1[...]

    give1 = [remote(S1, f1_ref.at[y, h], peer, home, home) for peer in y_peers]
    h2.wait_recv()
    S2[...] = (CY2[rows(64 * h, 64)].astype(F32) + RH2[...].astype(F32)).astype(BF)
    turn2 = turn(S2, A2)
    pair_v.wait_recv()
    LC[...] = LV[...] + LVX[...]
    LCR[chip] = LC[...]
    spread_v = [remote(LC, LCR.at[chip], chip_to(m)) for m in range(1, 8)]
    spread_sum(spread3, C3, R3, S3, 48)
    turn3 = turn(S3, A3)
    in_cores[3].wait_recv()
    in_x = scatter_x(in_z, DB, DRA, DRZ, DFX, DRX)
    arrived(give1)
    over1 = remote(f1_ref.at[:, h], f1_ref.at[:, h], h_peer, home, home)
    last1 = [remote(f1_ref.at[:, h], f1_ref.at[:, h], partner, home, off)]
    out_h2 = give_h(turn2, A2, f2_ref, 64)
    give3 = give(turn3, A3, f3_ref, 48)
    arrived(spread_v)
    total = LCR[0]
    for m in range(1, 8):
        total = total + LCR[m]
    v1_ref[...] = total[0:1].reshape(128)
    v2_ref[...] = total[1:2].reshape(128)
    v3_ref[...] = total[2:3].reshape(128)
    v4_ref[...] = total[3:4].reshape(128)
    vq_ref[...] = total[4:7].reshape(384)
    vu_ref[...] = total[8:12].reshape(512)
    vd_ref[...] = total[12:13].reshape(128)
    vw_ref[...] = total[12:13].reshape(128)

    give2 = give_y(out_h2, f2_ref, 64)
    scatter_end(in_x, DRX)
    block = OWNH[...].astype(F32)
    center = block - jnp.mean(block, axis=-1, keepdims=True)
    spread = jnp.mean(center * center, axis=-1, keepdims=True)
    scale = lax.rsqrt(spread + 1e-05)
    xhat = center * scale
    grad = ACC[...]
    grad = grad - jnp.mean(grad, axis=-1, keepdims=True) - xhat * jnp.mean(grad * xhat, axis=-1, keepdims=True)
    ing_ref[...] = (OWNG[...].astype(F32) + scale * grad).astype(BF)

    def flat(F, p, i, out, size):
        block = F[p, i].astype(F32)
        for j in range(size // 128):
            out_at = 128 * (2 * i + p) + 1024 * j if size == 384 else 512 * (2 * i + p) + 128 * j
            piece = jnp.transpose(block[128 * j : 128 * j + 128]).astype(BF)
            out[:, lanes(out_at, 128)] = piece

    arrived(give3)
    last3 = remote(f3_ref.at[k], f3_ref.at[k], partner)
    for i in range(4):
        flat(f3_ref, k, i, o3_ref, 384)
    over1.wait_recv()
    last1.append(remote(f1_ref.at[:, 1 - h], f1_ref.at[:, 1 - h], partner, home, off))
    arrived(give2)
    last2 = remote(f2_ref.at[k], f2_ref.at[k], partner)
    last3.wait_recv()
    for i in range(4):
        flat(f3_ref, 1 - k, i, o3_ref, 384)
    for i in range(4):
        flat(f2_ref, k, i, o2_ref, 512)
    last2.wait_recv()
    for i in range(4):
        flat(f2_ref, 1 - k, i, o2_ref, 512)
    arrived(last1)
    first = f1_ref[...].reshape(640, 1024)
    dn_ref[...] = first[0:512]
    de_ref[...] = first[512:640]
    for copy in sent:
        copy.wait_send()
    assert used[0] <= SEMS, used[0]


def block_call(*args):
    vm = pltpu.VMEM
    scratch = [
        vm((4, 2, 80, 1024), BF), vm((2, 4, 512, 128), BF), vm((2, 4, 384, 128), BF), vm((16, 128), F32), vm((8, 128), jnp.int32),
        vm((8, 8, 128), jnp.int32), vm((128, 1024), BF), vm((512, 1024), BF), vm((128, 1024), BF), vm((128, 1024), BF),
        vm((4, 2, 128, 1024), BF), vm((4, 2, 128, 1024), BF), vm((8, 8, 128), jnp.int32), vm((8, 16, 128), F32),
        vm((4, 2, 128, 384), BF), vm((4, 2, 128, 512), BF), vm((8, 1024), F32), vm((24, 128), F32),
        vm((1024, 1024), BF), vm((1024, 1024), BF), vm((1024, 1024), BF), vm((256, 1024), F32),
        vm((2, 8, 1024), F32), vm((8, 1024), jnp.int32),
        vm((2, 128, 1024), BF), vm((2, 1024, 128), BF), vm((128, 1024), BF), vm((1024, 128), BF),
        vm((1024, 128), BF), vm((128, 1024), BF),
        vm((1024, 512), F32), vm((1024, 512), BF), vm((512, 1024), BF), vm((2, 1024, 1024), BF),
        vm((128, 1024), BF), vm((1024, 128), BF), vm((2, 1024, 128), BF), vm((2, 128, 1024), BF),
        vm((1024, 512), BF), vm((512, 1024), BF), vm((128, 1024), F32), vm((1024, 128), F32), vm((1024, 128), F32),
        vm((1024, 384), BF), vm((384, 1024), BF),
    ]
    for _ in range(2):
        scratch += [
            vm((4, 2, 128, 1024), BF), vm((4, 128, 1024), BF), vm((3, 128, 1024), BF), vm((3, 128, 1024), BF),
            vm((128, 1024), BF), vm((128, 1024), BF),
        ]
    scratch += [vm((128, 1024), F32)]
    scratch += [
        vm((640, 1024), BF), vm((160, 1024), BF), vm((160, 1024), BF), vm((3, 160, 1024), BF), vm((80, 1024), BF),
        vm((160, 1024), BF), vm((80, 1024), BF),
    ]
    scratch += [
        vm((512, 1024), BF), vm((512, 512), BF), vm((512, 512), BF), vm((3, 128, 512), BF), vm((64, 512), BF),
        vm((128, 512), BF), vm((64, 512), BF), vm((4, 64, 128), BF),
        vm((384, 1024), BF), vm((384, 512), BF), vm((384, 512), BF), vm((7, 48, 512), BF), vm((48, 512), BF),
        vm((4, 48, 128), BF),
    ]
    scratch += [
        vm((4, 8, 1024), F32), vm((8, 1024), F32), vm((8, 512), F32), vm((8, 16, 128), F32), vm((7, 16, 128), F32),
        vm((16, 128), F32), vm((16, 128), F32), vm((16, 128), F32), vm((8, 16, 128), F32),
        pltpu.SemaphoreType.DMA((SEMS,)), pltpu.SemaphoreType.DMA((SEMS,)), pltpu.SemaphoreType.DMA((10,)),
    ]
    return pl.pallas_call(
        kernel,
        out_shape=(
            jax.ShapeDtypeStruct((128, 1024), BF), jax.ShapeDtypeStruct((128, 1024), BF),
            jax.ShapeDtypeStruct((512, 1024), BF), jax.ShapeDtypeStruct((128, 1024), BF),
            jax.ShapeDtypeStruct((128, 4096), BF),
            jax.ShapeDtypeStruct((128, 3072), BF),
        ) + tuple(jax.ShapeDtypeStruct((size,), F32) for size in (128, 128, 128, 128, 384, 128, 512, 128)),
        in_specs=[
            pl.BlockSpec(memory_space=pl.ANY if len(arg.shape) == 2 else pltpu.VMEM) for arg in args
        ],
        out_specs=[pl.BlockSpec(memory_space=pltpu.VMEM)] * 14,
        scratch_shapes=scratch,
        compiler_params=pltpu.CompilerParams(
            collective_id=0, has_side_effects=True, vmem_limit_bytes=62 * 2**20
        ),
    )(*args)


def shards(*args):
    out, ing, down, dense, up, qkv, v1, v2, v3, v4, vq, vd, vu, vw = block_call(*args)
    return (
        out, ing, v1, v2, v3, v4, qkv.astype(F32), vq, dense.astype(F32), vd, up.astype(F32), vu, down.astype(F32), vw,
    )


def solution(mesh):
    both, one, wide = P(("rep", "shard"), None), P("shard"), P("shard", None)
    placed = (
        both, both, P(("rep", "shard")), one, one, one, one, wide, one, wide, one, wide, one, wide, one,
    )
    return jax.shard_map(
        shards, mesh=mesh, in_specs=placed,
        out_specs=(both, both, one, one, one, one, wide, one, wide, one, wide, one, wide, one),
        check_vma=False,
    )
```

time: 133 us -> 125 us (0.940)
  Pallas kernels: 119 us -> 112 us
  local copies, waits for them, and re-layouts: 10.4 us -> 5.68 us
  other arithmetic: 2.82 us -> 6.55 us
    pallas_call x1, Pallas kernels: 119 us -> 112 us  [block_call(): pl.pallas_call(kernel, out_shape=(jax.ShapeDtypeStruct((128, 1024), BF),...]
    slice x2 -> x0, local copies, waits for them, and re-layouts: 4.74 us -> none  [the longest x1 2.88 us: shards(): first[0:512]]
    convert_element_type x0 -> x2, other arithmetic: none -> 2.41 us  [the longest x1 1.57 us: shards(): down.astype(F32)]
    unnamed x34 -> x36, local copies, waits for them, and re-layouts: 5.68 us -> 5.68 us
where the time goes in v3:
time: 125 us
  Pallas kernels  112 us (90%)
  other arithmetic  6.55 us (5%)
  local copies, waits for them, and re-layouts  5.68 us (5%)
    pallas_call x1, Pallas kernels, block_call(): pl.pallas_call(kernel, out_shape=(jax.ShapeDtypeStruct((128, 1024), BF),...  112 us
    unnamed x36, local copies, waits for them, and re-layouts  5.68 us
    convert_element_type x1, other arithmetic, shards(): up.astype(F32)  2.84 us

profile of v3, /device:TPU:1, one launch (start us, length us, event | category | flops | bytes accessed | tf_op | source)
XLA Modules:
  0.0 124.6 jit_solution(5580846343595720353)
XLA Ops:
  0.7 111.6 %shard_map.254 = (bf16[128,1024]{1,0:T(8,128)(2,1)}, bf16[128,1024]{1,0:T(8,128)(2,1)}, bf16[512,1024]{1,0:T(8,128)(2,1)}, bf16[128,1024]{1,0:T(8,128)(2,1)}, bf...) custom-call(bf16[128,1024]{1,0:T(8,128)(2,1)} %hid_ref.1, ...), custom_call_target="tpu_custom_call" | custom-call | tf_op jit(solution)/shard_map/pallas_call | solution.py:708
  112.3 0.0 copy-start
  112.3 2.8 %convert_element_type.14 = f32[128,4096]{1,0:T(8,128)} convert(bf16[128,4096]{1,0:T(8,128)(2,1)} %get-tuple-element.38) | non-fusion elementwise | flops 524288 | bytes 3145728 | tf_op jit(solution)/shard_map/convert_element_type | solution.py:730
  115.1 0.0 copy-done
  115.1 1.6 %convert_element_type.15 = f32[512,1024]{1,0:T(8,128)} convert(bf16[512,1024]{1,0:T(8,128)(2,1)S(1)} %copy-done) | non-fusion elementwise | flops 524288 | bytes 3145728 | tf_op jit(solution)/shard_map/convert_element_type | solution.py:730
  116.7 0.0 copy-done.1
  116.7 0.0 copy-start.11
  116.7 0.0 copy-start.10
  116.7 0.0 copy-start.9
  116.7 0.0 copy-start.6
  116.7 0.0 copy-start.8
  116.7 0.0 copy-start.5
  116.8 0.0 copy-start.7
  116.8 1.3 %convert_element_type.12 = f32[128,3072]{1,0:T(8,128)} convert(bf16[128,3072]{1,0:T(8,128)(2,1)S(1)} %copy-done.1) | non-fusion elementwise | flops 393216 | bytes 2359296 | tf_op jit(solution)/shard_map/convert_element_type | solution.py:730
  118.1 0.0 copy-done.2
  118.1 0.8 convert_element_type.13
  118.9 0.0 copy-done.4
  118.9 0.7 copy.39
  119.6 0.0 copy-done.3
  119.6 0.7 copy.40
  120.3 0.5 copy.41
  120.8 0.0 copy-done.11
  120.8 0.5 copy.42
  121.4 0.0 copy-done.10
  121.4 0.5 copy.43
  121.9 0.5 copy.44
  122.4 0.6 copy.45
  123.0 0.0 copy-done.8
  123.0 0.5 copy.46
  123.5 0.6 copy.47
  124.1 0.0 copy-done.7
  124.1 0.5 copy.48
  (9 shorter events, 0.0 us)
Async XLA Ops:
  112.3 2.9 %copy-start = (bf16[512,1024]{1,0:T(8,128)(2,1)S(1)}, bf16[512,1024]{1,0:T(8,128)(2,1)}, u32[]{:S(2)}) copy-start(bf16[512,1024]{1,0:T(8,128)(2,1)} %get-tuple-element.40) | copy-start | bytes 3145732
  115.1 1.6 %copy-start.1 = (bf16[128,3072]{1,0:T(8,128)(2,1)S(1)}, bf16[128,3072]{1,0:T(8,128)(2,1)}, u32[]{:S(2)}) copy-start(bf16[128,3072]{1,0:T(8,128)(2,1)} %get-tuple-element.34) | copy-start | bytes 2359300
  115.1 2.9 %copy-start.2 = (bf16[128,1024]{1,0:T(8,128)(2,1)S(1)}, bf16[128,1024]{1,0:T(8,128)(2,1)}, u32[]{:S(2)}) copy-start(bf16[128,1024]{1,0:T(8,128)(2,1)} %get-tuple-element.36) | copy-start | bytes 786436
  116.7 2.2 %copy-start.4 = (bf16[128,1024]{1,0:T(8,128)(2,1)S(1)}, bf16[128,1024]{1,0:T(8,128)(2,1)}, u32[]{:S(2)}) copy-start(bf16[128,1024]{1,0:T(8,128)(2,1)} %get-tuple-element.56) | copy-start | bytes 786436
  116.7 2.9 %copy-start.3 = (bf16[128,1024]{1,0:T(8,128)(2,1)S(1)}, bf16[128,1024]{1,0:T(8,128)(2,1)}, u32[]{:S(2)}) copy-start(bf16[128,1024]{1,0:T(8,128)(2,1)} %get-tuple-element.57) | copy-start | bytes 786436
  116.7 3.6 %copy-start.12 = (f32[128]{0:T(128)S(1)}, f32[128]{0:T(128)}, u32[]{:S(2)}) copy-start(f32[128]{0:T(128)} %get-tuple-element.58) | copy-start | bytes 1540
  116.7 4.1 %copy-start.11 = (f32[128]{0:T(128)S(1)}, f32[128]{0:T(128)}, u32[]{:S(2)}) copy-start(f32[128]{0:T(128)} %get-tuple-element.59) | copy-start | bytes 1540
  116.7 4.6 %copy-start.10 = (f32[128]{0:T(128)S(1)}, f32[128]{0:T(128)}, u32[]{:S(2)}) copy-start(f32[128]{0:T(128)} %get-tuple-element.60) | copy-start | bytes 1540
  116.7 5.2 %copy-start.9 = (f32[128]{0:T(128)S(1)}, f32[128]{0:T(128)}, u32[]{:S(2)}) copy-start(f32[128]{0:T(128)} %get-tuple-element.61) | copy-start | bytes 1540
  116.7 5.7 %copy-start.6 = (f32[384]{0:T(512)S(1)}, f32[384]{0:T(512)}, u32[]{:S(2)}) copy-start(f32[384]{0:T(512)} %get-tuple-element.63) | copy-start | bytes 4612
  116.7 6.2 %copy-start.8 = (f32[128]{0:T(128)S(1)}, f32[128]{0:T(128)}, u32[]{:S(2)}) copy-start(f32[128]{0:T(128)} %get-tuple-element.65) | copy-start | bytes 1540
  116.7 6.7 %copy-start.5 = (f32[512]{0:T(512)S(1)}, f32[512]{0:T(512)}, u32[]{:S(2)}) copy-start(f32[512]{0:T(512)} %get-tuple-element.67) | copy-start | bytes 6148
  116.8 7.3 %copy-start.7 = (f32[128]{0:T(128)S(1)}, f32[128]{0:T(128)}, u32[]{:S(2)}) copy-start(f32[128]{0:T(128)} %get-tuple-element.69) | copy-start | bytes 1540

commit v4 on v3

--- a/solution.py
+++ b/solution.py
@@ -38,12 +38,11 @@
 def kernel(
     hid_ref, g_ref, seg_ref, gain1_ref, shift1_ref, gain2_ref, shift2_ref, wqkv_ref, bqkv_ref, wdense_ref,
     bdense_ref, wup_ref, bup_ref, wdown_ref, bdown_ref,
-    out_ref, ing_ref, dn_ref, de_ref, o2_ref, o3_ref, v1_ref, v2_ref, v3_ref, v4_ref, vq_ref, vd_ref, vu_ref, vw_ref,
-    f1_ref, f2_ref, f3_ref, PKO, SGO, SGX, WD, WN, OWNH, OWNG,
+    out_ref, ing_ref, f1_ref, f2_ref, f3_ref, vec_ref, PKO, SGO, SGX, WD, WN, OWNH, OWNG,
     HB, GB, SG, PK, WQ, WU, VEC, B24, XH, N1, N2, QKP, TAB, START, QTM, QM, KT, K, V, VT,
     GP, ACT, ACTT, PT, CTXT, CTX, DCM, DCTM, DG, DGT, DQT, DK, DV, M, MT,
     PB, PRA, PRT, PRZ, PFX, PRX, DB, DRA, DRT, DRZ, DFX, DRX, ACC,
-    G1, X1, C1, R1, S1, CY1, RH1, G2, X2, C2, R2, S2, CY2, RH2, A2, G3, X3, C3, R3, S3, A3,
+    G1, X1, R1, S1, CY1, G2, X2, C2, R2, S2, G3, X3, C3, R3, S3,
     SUMS, CG, CDG, SV, SVR, LV, LVX, LC, LCR,
     ssem, rsem, lsem,
 ):
@@ -83,6 +82,7 @@
 
     barrier = pltpu.get_barrier_semaphore()
     peers = [shard_to(m) for m in range(1, 8)] + [chip_to(m) for m in range(1, 8)] + [partner, x_far, x_cross]
+    peers += [{"rep": (4 * (1 - h) + y) * 2 + k, "shard": 2 * zz + l} for zz in zs]
     for peer in peers:
         pl.semaphore_signal(barrier, inc=1, device_id=peer, device_id_type=MESH)
 
@@ -187,6 +187,18 @@
         cores.append(same(XB.at[ahead, k], partner))
         return XB, d2a, d2b, cores
 
+    def gather_straight(first, XB):
+        first.wait_recv()
+        own = XB.at[z, k]
+        return [same(own, z_to(zz)) for zz in (across_z, ahead, behind)], [same(own, partner)]
+
+    def gather_core(state, XB):
+        copies, cores = state
+        for copy, zz in zip(copies, (across_z, behind, ahead)):
+            copy.wait_recv()
+            cores.append(same(XB.at[zz, k], partner))
+        return cores
+
     def gather_last(state):
         XB, d2a, d2b, cores = state
         arrived([d2a, d2b])
@@ -208,41 +220,35 @@
     near32 = rows(32 * y, 16)
     far32 = rows(32 * y + 16, 16)
     both32 = rows(32 * y, 32)
-    both128 = rows(128 * y, 128)
     gather_h = gather_x(hid_ref, HB)
     up_z = [
         remote(wup_ref.at[both32, lanes(512 * (2 * zz + k), 512)], WU.at[z, l, both32], z_to(zz))
         for zz in (ahead, behind, across_z)
     ]
-    outer_x = [
-        remote(wdown_ref.at[rows(128 * y, 64)], WN.at[rows(128 * y, 64)], x_near, home, off),
-        remote(wdown_ref.at[rows(128 * y + 64, 64)], WN.at[rows(128 * y + 64, 64)], x_far, home, off),
-        remote(wdense_ref.at[near32], WD.at[near32], x_near, home, off),
-        remote(wdense_ref.at[far32], WD.at[far32], x_far, home, off),
-    ]
     qkv_z = weight_z(wqkv_ref, WQ, 128, 3)
     qkv_x = weight_x(WQ, z)
+    gather_g = gather_x(g_ref, GB)
     gather_h = gather_z(gather_h, HB)
     small = [remote(PKO, PK.at[s], shard_to(m)) for m in range(1, 8)]
     small += [remote(SGO, SG.at[s], shard_to(m)) for m in range(1, 8)]
     arrived(up_z)
     up_x = [same(WU.at[:, l, near32], x_near), same(WU.at[:, l, far32], x_far)]
-    arrived(outer_x)
-    outer_y = [
-        remote(ref.at[part], ref.at[part], peer, off, off)
-        for peer in y_peers for ref, part in ((WN, both128), (WD, both32))
-    ]
     for copies, zz in zip(qkv_z, (behind, ahead, across_z)):
         arrived(copies)
         qkv_x += weight_x(WQ, zz)
     arrived(up_x)
     up_y = [same(WU.at[:, :, both32], peer) for peer in y_peers]
     gather_h = gather_next(gather_h)
-    gather_g = gather_x(g_ref, GB)
+    gather_g = gather_straight(gather_g, GB)
+    outer = [
+        remote(wdown_ref.at[0:256], WN.at[0:256], x_near, home, off),
+        remote(wdown_ref.at[256:512], WN.at[256:512], x_far, home, off),
+        remote(wdense_ref.at[low], WD.at[low], x_near, home, off),
+        remote(wdense_ref.at[high], WD.at[high], x_far, home, off),
+    ]
     arrived(small)
     seg_core = remote(SG, SGX, partner)
     rest_h = gather_last(gather_h)
-    gather_g = gather_z(gather_g, GB)
 
     for sp in range(8):
         block = PK[sp]
@@ -272,14 +278,12 @@
     TAB[1] = jnp.sin(angles)
     gain1, shift1, gain2, shift2 = (VEC[j : j + 1] for j in range(4))
 
-    arrived(rest_h)
     arrived(qkv_x)
 
-    @pl.loop(0, 4)
-    def _(i):
-        at = rows(256 * i, 256)
-        cols = lanes(256 * i, 256)
-        block = HB[i].reshape(256, 1024).astype(F32)
+    def project(zz):
+        at = rows(256 * zz, 256)
+        cols = lanes(256 * zz, 256)
+        block = HB[zz].reshape(256, 1024).astype(F32)
         center = block - jnp.mean(block, axis=-1, keepdims=True)
         spread = jnp.mean(center * center, axis=-1, keepdims=True)
         xhat = center * lax.rsqrt(spread + 1e-05)
@@ -291,6 +295,10 @@
         QKP[:, cols] = jnp.transpose(mixed[:, :256])
         V[at] = mixed[:, 256:].astype(BF)
         VT[:, cols] = jnp.transpose(mixed[:, 256:]).astype(BF)
+
+    for copy, zz in zip(rest_h, (z, behind, ahead, across_z)):
+        copy.wait_recv()
+        project(zz)
 
     cosine = TAB[0]
     sine = TAB[1]
@@ -327,7 +335,6 @@
             CTXT[hr, q] = nn(VT[hr, 0:top], probs).astype(BF)
 
     attention(0)
-    gather_g = gather_next(gather_g)
     attention(1)
 
     def scatter_core(TB, RA):
@@ -359,9 +366,9 @@
             ACC[...] = RX[...].astype(F32)
 
     CTX[...] = jnp.transpose(CTXT[...].astype(F32)).astype(BF)
-    rest_g = gather_last(gather_g)
+    rest_g = gather_core(gather_g, GB)
     arrived(up_y)
-    arrived(outer_y)
+    arrived(outer)
 
     @pl.loop(0, 4)
     def _(i):
@@ -390,12 +397,14 @@
         arrived(near)
         C[...] = (GR[:, lanes(512 * l, 512)].astype(F32) + X[...].astype(F32)).astype(BF)
         return [
-            remote(C.at[rows(size * flip(chip, m), size)], R.at[m - 1], chip_to(m)) for m in range(1, 8)
+            remote(
+                C.at[rows(size * (2 * flip(y, m % 4) + flip(h, m // 4)), size)], R.at[m - 1], chip_to(m))
+            for m in range(1, 8)
         ]
 
     def spread_sum(copies, C, R, S, size):
         arrived(copies)
-        total = C[rows(size * chip, size)].astype(F32)
+        total = C[rows(size * (2 * y + h), size)].astype(F32)
         for m in range(7):
             total = total + R[m].astype(F32)
         S[...] = total.astype(BF)
@@ -403,40 +412,33 @@
     y_at = [flip(y, m) for m in (1, 3, 2)]
     h_peer = {"rep": (4 * (1 - h) + y) * 2 + k}
 
-    def along_y(C, R, size, role=None):
-        return [
-            remote(C.at[rows(2 * size * yy, 2 * size)], R.at[m], y_peers[m], role, role) for m, yy in enumerate(y_at)
-        ]
-
-    def quarter_sum(copies, C, R, CY, size):
+    def along_y(C, R, size):
+        return [remote(C.at[rows(2 * size * yy, 2 * size)], R.at[m], y_peers[m]) for m, yy in enumerate(y_at)]
+
+    def turn(S, out, size):
+        at = rows(size * (2 * y + h), size)
+        out[k, z, at] = S[:, lanes(128 * z, 128)]
+        copies = []
+        for zz in (across_z, ahead, behind, z):
+            source = S.at[:, lanes(128 * zz, 128)]
+            copies.append(remote(source, out.at[k, z, at], {"rep": (4 * (1 - h) + y) * 2 + k, "shard": 2 * zz + l}))
+        for zz in (ahead, behind, across_z):
+            copies.append(remote(S.at[:, lanes(128 * zz, 128)], out.at[k, z, at], z_to(zz)))
+        return copies
+
+    def quarter(out, yy, size):
+        return out.at[k, :, rows(2 * size * yy, 2 * size)]
+
+    def give_y(copies, out, size):
         arrived(copies)
-        CY[...] = (
-            C[rows(2 * size * y, 2 * size)].astype(F32) + R[0].astype(F32) + R[1].astype(F32) + R[2].astype(F32)
-        ).astype(BF)
-
-    def along_h(CY, RH, size, role=None):
-        return remote(CY.at[rows(size * (1 - h), size)], RH, h_peer, role, role)
-
-    def turn(S, A):
-        A[z] = S[:, lanes(128 * z, 128)]
-        return [remote(S.at[:, lanes(128 * zz, 128)], A.at[z], z_to(zz)) for zz in (ahead, behind, across_z)]
-
-    def give(copies, A, out, size):
-        arrived(copies)
-        at = rows(size * chip, size)
-        out[k, :, at] = A[...]
-        return [remote(A, out.at[k, :, at], chip_to(m)) for m in range(1, 8)]
-
-    def give_h(copies, A, out, size):
-        arrived(copies)
-        at = rows(size * (2 * y + h), size)
-        out[k, :, at] = A[...]
-        return remote(A, out.at[k, :, at], h_peer)
-
-    def give_y(copy, out, size):
-        copy.wait_recv()
-        ref = out.at[k, :, rows(2 * size * y, 2 * size)]
-        return [remote(ref, ref, peer) for peer in y_peers]
+        return [remote(quarter(out, y, size), quarter(out, y, size), peer) for peer in y_peers]
+
+    def give_core(copies, out, size):
+        last = [same(quarter(out, y, size), partner)]
+        for copy, yy in zip(copies, y_at):
+            copy.wait_recv()
+            last.append(same(quarter(out, yy, size), partner))
+        return last
 
     def put(GR, total):
         for sp in range(8):
@@ -447,25 +449,6 @@
     G1[0:512] = nn(ACTT[...], grads).astype(BF)
     G1[512:640] = nn(CTXT[...], grads).astype(BF)
     y1 = along_y(G1, R1, 80)
-
-    CG[...] = jnp.zeros_like(CG)
-    CDG[...] = jnp.zeros_like(CDG)
-
-    @pl.loop(0, 4)
-    def _(i):
-        at = rows(256 * i, 256)
-        cols = lanes(256 * i, 256)
-        block = GB[i].reshape(256, 1024)
-        CG[...] += fold(block.astype(F32))
-        gate_grad = (nt(block, WN[...]) * GP[at]).astype(BF)
-        DG[at] = gate_grad
-        wide = gate_grad.astype(F32)
-        CDG[...] += fold(wide)
-        DGT[:, cols] = jnp.transpose(wide).astype(BF)
-
-    out_z = scatter_z(out_cores, PB, PRA, PRT, PRZ)
-    put(G2, nn(DGT[...], N2[...]))
-    near2 = near_start(G2, X2, 64)
 
     low_256 = lax.broadcasted_iota(jnp.int32, (256, 128), 1) < 64
     low_t256 = lax.broadcasted_iota(jnp.int32, (128, 256), 0) < 64
@@ -499,10 +482,8 @@
             DV[0:top] += nn(probs, DCM[head, q])
 
     attention_back(0)
+    out_z = scatter_z(out_cores, PB, PRA, PRT, PRZ)
     attention_back(1)
-    arrived(near2)
-    C2[...] = (G2[:, lanes(512 * l, 512)].astype(F32) + X2[...].astype(F32)).astype(BF)
-    y2 = along_y(C2, R2, 64)
 
     QKP[0:128] = DQT[...]
     QKP[128:256] = jnp.transpose(DK[...])
@@ -518,6 +499,24 @@
     near3 = near_start(G3, X3, 48)
     M[:, 0:256] = jnp.transpose(QKP[...]).astype(BF)
     M[:, 256:384] = DV[...].astype(BF)
+    CG[...] = jnp.zeros_like(CG)
+    CDG[...] = jnp.zeros_like(CDG)
+
+    @pl.loop(0, 4)
+    def _(i):
+        at = rows(256 * i, 256)
+        cols = lanes(256 * i, 256)
+        block = GB[i].reshape(256, 1024)
+        CG[...] += fold(block.astype(F32))
+        gate_grad = (nt(block, WN[...]) * GP[at]).astype(BF)
+        DG[at] = gate_grad
+        wide = gate_grad.astype(F32)
+        CDG[...] += fold(wide)
+        DGT[:, cols] = jnp.transpose(wide).astype(BF)
+
+    put(G2, nn(DGT[...], N2[...]))
+    near2 = near_start(G2, X2, 64)
+
     SUMS[...] = jnp.zeros_like(SUMS)
     in_cores = []
     in_z = []
@@ -541,17 +540,22 @@
         in_z.append(remote(DRT.at[j], DRZ.at[j], z_to(zz)))
 
     norm_grads(across_z)
+    spread3 = spread_start(near3, G3, X3, C3, R3, 48)
     norm_grads(ahead)
     norm_send(0)
-    quarter_sum(y1, G1, R1, CY1, 80)
-    near1 = [
-        remote(CY1.at[0:80], X1.at[0:80], x_near, off, home),
-        remote(CY1.at[80:160], X1.at[80:160], x_far, off, home),
-    ]
     norm_grads(behind)
     norm_send(1)
     norm_grads(z)
     norm_send(2)
+    arrived(y1)
+    CY1[...] = (
+        G1[rows(160 * y, 160)].astype(F32) + R1[0].astype(F32) + R1[1].astype(F32) + R1[2].astype(F32)
+    ).astype(BF)
+    x1 = [
+        remote(CY1.at[rows(80 * h, 80)], X1.at[0], x_near, off, home),
+        remote(CY1.at[rows(80 * (1 - h), 80)], X1.at[1], x_far, off, home),
+        remote(CY1.at[rows(80 * (1 - h), 80)], X1.at[2], h_peer, home, home),
+    ]
     out_x = scatter_x(out_z, PB, PRA, PRZ, PFX, PRX)
 
     SV[...] = jnp.zeros_like(SV)
@@ -570,62 +574,41 @@
     SV[b, 12:13] = jnp.sum(CG[:, lanes(128 * b, 128)], axis=0, keepdims=True)
     vectors = [remote(SV.at[flip(s, m)], SVR.at[m - 1], shard_to(m)) for m in range(1, 8)]
 
-    spread3 = spread_start(near3, G3, X3, C3, R3, 48)
-    quarter_sum(y2, C2, R2, CY2, 64)
-    h2 = along_h(CY2, RH2, 64)
-    arrived(near1)
+    spread2 = spread_start(near2, G2, X2, C2, R2, 64)
+    spread_sum(spread3, C3, R3, S3, 48)
+    turn3 = turn(S3, f3_ref, 48)
+    arrived(x1)
 
     @pl.when(home)
     def _():
-        C1[...] = (CY1[...].astype(F32) + X1[...].astype(F32)).astype(BF)
-
-    h1 = along_h(C1, RH1, 80, home)
+        S1[...] = (
+            CY1[rows(80 * h, 80)].astype(F32) + X1[0].astype(F32) + X1[1].astype(F32) + X1[2].astype(F32)
+        ).astype(BF)
+        f1_ref[y, h] = S1[...]
+
+    give1 = [remote(S1, f1_ref.at[y, h], chip_to(m), home, home) for m in range(1, 8)]
     scatter_end(out_x, PRX)
     out_ref[...] = (OWNH[...].astype(F32) + ACC[...] + VEC[4:5]).astype(BF)
+    give3 = give_y(turn3, f3_ref, 48)
     arrived(vectors)
     total = SV[s]
     for m in range(7):
         total = total + SVR[m]
     LV[...] = total
     pair_v = remote(LV, LVX, partner)
-    h1.wait_recv()
-
-    @pl.when(home)
-    def _():
-        S1[...] = (C1[rows(80 * h, 80)].astype(F32) + RH1[...].astype(F32)).astype(BF)
-        f1_ref[y, h] = S1[...]
-
-    give1 = [remote(S1, f1_ref.at[y, h], peer, home, home) for peer in y_peers]
-    h2.wait_recv()
-    S2[...] = (CY2[rows(64 * h, 64)].astype(F32) + RH2[...].astype(F32)).astype(BF)
-    turn2 = turn(S2, A2)
+    spread_sum(spread2, C2, R2, S2, 64)
+    turn2 = turn(S2, f2_ref, 64)
+    in_cores[3].wait_recv()
+    in_x = scatter_x(in_z, DB, DRA, DRZ, DFX, DRX)
     pair_v.wait_recv()
     LC[...] = LV[...] + LVX[...]
     LCR[chip] = LC[...]
     spread_v = [remote(LC, LCR.at[chip], chip_to(m)) for m in range(1, 8)]
-    spread_sum(spread3, C3, R3, S3, 48)
-    turn3 = turn(S3, A3)
-    in_cores[3].wait_recv()
-    in_x = scatter_x(in_z, DB, DRA, DRZ, DFX, DRX)
+    give2 = give_y(turn2, f2_ref, 64)
     arrived(give1)
-    over1 = remote(f1_ref.at[:, h], f1_ref.at[:, h], h_peer, home, home)
-    last1 = [remote(f1_ref.at[:, h], f1_ref.at[:, h], partner, home, off)]
-    out_h2 = give_h(turn2, A2, f2_ref, 64)
-    give3 = give(turn3, A3, f3_ref, 48)
-    arrived(spread_v)
-    total = LCR[0]
-    for m in range(1, 8):
-        total = total + LCR[m]
-    v1_ref[...] = total[0:1].reshape(128)
-    v2_ref[...] = total[1:2].reshape(128)
-    v3_ref[...] = total[2:3].reshape(128)
-    v4_ref[...] = total[3:4].reshape(128)
-    vq_ref[...] = total[4:7].reshape(384)
-    vu_ref[...] = total[8:12].reshape(512)
-    vd_ref[...] = total[12:13].reshape(128)
-    vw_ref[...] = total[12:13].reshape(128)
-
-    give2 = give_y(out_h2, f2_ref, 64)
+    last1 = [remote(f1_ref, f1_ref, partner, home, off)]
+    last3 = give_core(give3, f3_ref, 48)
+
     scatter_end(in_x, DRX)
     block = OWNH[...].astype(F32)
     center = block - jnp.mean(block, axis=-1, keepdims=True)
@@ -636,33 +619,15 @@
     grad = grad - jnp.mean(grad, axis=-1, keepdims=True) - xhat * jnp.mean(grad * xhat, axis=-1, keepdims=True)
     ing_ref[...] = (OWNG[...].astype(F32) + scale * grad).astype(BF)
 
-    def flat(F, p, i, out, size):
-        block = F[p, i].astype(F32)
-        for j in range(size // 128):
-            out_at = 128 * (2 * i + p) + 1024 * j if size == 384 else 512 * (2 * i + p) + 128 * j
-            piece = jnp.transpose(block[128 * j : 128 * j + 128]).astype(BF)
-            out[:, lanes(out_at, 128)] = piece
-
-    arrived(give3)
-    last3 = remote(f3_ref.at[k], f3_ref.at[k], partner)
-    for i in range(4):
-        flat(f3_ref, k, i, o3_ref, 384)
-    over1.wait_recv()
-    last1.append(remote(f1_ref.at[:, 1 - h], f1_ref.at[:, 1 - h], partner, home, off))
-    arrived(give2)
-    last2 = remote(f2_ref.at[k], f2_ref.at[k], partner)
-    last3.wait_recv()
-    for i in range(4):
-        flat(f3_ref, 1 - k, i, o3_ref, 384)
-    for i in range(4):
-        flat(f2_ref, k, i, o2_ref, 512)
-    last2.wait_recv()
-    for i in range(4):
-        flat(f2_ref, 1 - k, i, o2_ref, 512)
+    arrived(spread_v)
+    total = LCR[0]
+    for m in range(1, 8):
+        total = total + LCR[m]
+    vec_ref[...] = total
+    last2 = give_core(give2, f2_ref, 64)
     arrived(last1)
-    first = f1_ref[...].reshape(640, 1024)
-    dn_ref[...] = first[0:512]
-    de_ref[...] = first[512:640]
+    arrived(last2)
+    arrived(last3)
     for copy in sent:
         copy.wait_send()
     assert used[0] <= SEMS, used[0]
@@ -671,7 +636,7 @@
 def block_call(*args):
     vm = pltpu.VMEM
     scratch = [
-        vm((4, 2, 80, 1024), BF), vm((2, 4, 512, 128), BF), vm((2, 4, 384, 128), BF), vm((16, 128), F32), vm((8, 128), jnp.int32),
+        vm((16, 128), F32), vm((8, 128), jnp.int32),
         vm((8, 8, 128), jnp.int32), vm((128, 1024), BF), vm((512, 1024), BF), vm((128, 1024), BF), vm((128, 1024), BF),
         vm((4, 2, 128, 1024), BF), vm((4, 2, 128, 1024), BF), vm((8, 8, 128), jnp.int32), vm((8, 16, 128), F32),
         vm((4, 2, 128, 384), BF), vm((4, 2, 128, 512), BF), vm((8, 1024), F32), vm((24, 128), F32),
@@ -691,14 +656,11 @@
         ]
     scratch += [vm((128, 1024), F32)]
     scratch += [
-        vm((640, 1024), BF), vm((160, 1024), BF), vm((160, 1024), BF), vm((3, 160, 1024), BF), vm((80, 1024), BF),
-        vm((160, 1024), BF), vm((80, 1024), BF),
+        vm((640, 1024), BF), vm((3, 80, 1024), BF), vm((3, 160, 1024), BF), vm((80, 1024), BF), vm((160, 1024), BF),
     ]
     scratch += [
-        vm((512, 1024), BF), vm((512, 512), BF), vm((512, 512), BF), vm((3, 128, 512), BF), vm((64, 512), BF),
-        vm((128, 512), BF), vm((64, 512), BF), vm((4, 64, 128), BF),
+        vm((512, 1024), BF), vm((512, 512), BF), vm((512, 512), BF), vm((7, 64, 512), BF), vm((64, 512), BF),
         vm((384, 1024), BF), vm((384, 512), BF), vm((384, 512), BF), vm((7, 48, 512), BF), vm((48, 512), BF),
-        vm((4, 48, 128), BF),
     ]
     scratch += [
         vm((4, 8, 1024), F32), vm((8, 1024), F32), vm((8, 512), F32), vm((8, 16, 128), F32), vm((7, 16, 128), F32),
@@ -709,14 +671,13 @@
         kernel,
         out_shape=(
             jax.ShapeDtypeStruct((128, 1024), BF), jax.ShapeDtypeStruct((128, 1024), BF),
-            jax.ShapeDtypeStruct((512, 1024), BF), jax.ShapeDtypeStruct((128, 1024), BF),
-            jax.ShapeDtypeStruct((128, 4096), BF),
-            jax.ShapeDtypeStruct((128, 3072), BF),
-        ) + tuple(jax.ShapeDtypeStruct((size,), F32) for size in (128, 128, 128, 128, 384, 128, 512, 128)),
+            jax.ShapeDtypeStruct((4, 2, 80, 1024), BF), jax.ShapeDtypeStruct((2, 4, 512, 128), BF),
+            jax.ShapeDtypeStruct((2, 4, 384, 128), BF), jax.ShapeDtypeStruct((16, 128), F32),
+        ),
         in_specs=[
             pl.BlockSpec(memory_space=pl.ANY if len(arg.shape) == 2 else pltpu.VMEM) for arg in args
         ],
-        out_specs=[pl.BlockSpec(memory_space=pltpu.VMEM)] * 14,
+        out_specs=[pl.BlockSpec(memory_space=pltpu.VMEM)] * 6,
         scratch_shapes=scratch,
         compiler_params=pltpu.CompilerParams(
             collective_id=0, has_side_effects=True, vmem_limit_bytes=62 * 2**20
@@ -724,11 +685,90 @@
     )(*args)
 
 
+def finish(
+    out_in, ing_in, f1_in, f2_in, f3_in, vec_ref,
+    out_ref, ing_ref, v1_ref, v2_ref, v3_ref, v4_ref, qkv_ref, vq_ref, dense_ref, vd_ref, up_ref, vu_ref, down_ref,
+    vw_ref, B1, B2, B3, B4, B5, O1, O2, O3, sems,
+):
+    take = [
+        pltpu.make_async_copy(f3_in, B3, sems.at[0]),
+        pltpu.make_async_copy(f2_in, B2, sems.at[1]),
+        pltpu.make_async_copy(f1_in, B1, sems.at[2]),
+        pltpu.make_async_copy(out_in, B4, sems.at[3]),
+        pltpu.make_async_copy(ing_in, B5, sems.at[4]),
+    ]
+    for copy in take:
+        copy.start()
+    for ref, at in (
+        (v1_ref, 0), (v2_ref, 1), (v3_ref, 2), (v4_ref, 3), (vq_ref, 4), (vu_ref, 8), (vd_ref, 12), (vw_ref, 12)
+    ):
+        size = ref.shape[0]
+        ref[...] = vec_ref[at : at + size // 128].reshape(size)
+    put = []
+
+    def give(source, target):
+        copy = pltpu.make_async_copy(source, target, sems.at[5 + len(put)])
+        copy.start()
+        put.append(copy)
+
+    take[0].wait()
+    for j in range(3):
+        for sp in range(8):
+            at = 1024 * j + 128 * sp
+            O3[:, at : at + 128] = jnp.transpose(B3[sp % 2, sp // 2, 128 * j : 128 * j + 128].astype(F32))
+        part = slice(1024 * j, 1024 * j + 1024)
+        give(O3.at[:, part], qkv_ref.at[:, part])
+    take[1].wait()
+    for sp in range(8):
+        for j in range(4):
+            at = 512 * sp + 128 * j
+            O2[:, at : at + 128] = jnp.transpose(B2[sp % 2, sp // 2, 128 * j : 128 * j + 128].astype(F32))
+        if sp % 2:
+            part = slice(512 * sp - 512, 512 * sp + 512)
+            give(O2.at[:, part], up_ref.at[:, part])
+    take[3].wait()
+    give(B4, out_ref)
+    take[4].wait()
+    give(B5, ing_ref)
+    take[2].wait()
+    for j in range(4):
+        O1[160 * j : 160 * j + 160] = B1[j].astype(F32).reshape(160, 1024)
+        if j < 3:
+            give(O1.at[160 * j : 160 * j + 160], down_ref.at[160 * j : 160 * j + 160])
+    give(O1.at[480:512], down_ref.at[480:512])
+    give(O1.at[512:640], dense_ref)
+    for copy in put:
+        copy.wait()
+
+
 def shards(*args):
-    out, ing, down, dense, up, qkv, v1, v2, v3, v4, vq, vd, vu, vw = block_call(*args)
-    return (
-        out, ing, v1, v2, v3, v4, qkv.astype(F32), vq, dense.astype(F32), vd, up.astype(F32), vu, down.astype(F32), vw,
-    )
+    given = block_call(*args)
+    vm = pltpu.VMEM
+    any_, whole = pl.BlockSpec(memory_space=pl.ANY), pl.BlockSpec(memory_space=vm)
+
+    def flat(size):
+        return jax.ShapeDtypeStruct((size,), F32)
+
+    def wide(rows, columns, kind=F32):
+        return jax.ShapeDtypeStruct((rows, columns), kind)
+
+    return pl.pallas_call(
+        finish,
+        out_shape=(
+            wide(128, 1024, BF), wide(128, 1024, BF), flat(128), flat(128), flat(128), flat(128), wide(128, 3072),
+            flat(384), wide(128, 1024), flat(128), wide(128, 4096), flat(512), wide(512, 1024), flat(128),
+        ),
+        in_specs=[any_] * 5 + [whole],
+        out_specs=[
+            any_, any_, whole, whole, whole, whole, any_, whole, any_, whole, any_, whole, any_, whole,
+        ],
+        scratch_shapes=[
+            vm((4, 2, 80, 1024), BF), vm((2, 4, 512, 128), BF), vm((2, 4, 384, 128), BF),
+            vm((128, 1024), BF), vm((128, 1024), BF), vm((640, 1024), F32),
+            vm((128, 4096), F32), vm((128, 3072), F32), pltpu.SemaphoreType.DMA((20,)),
+        ],
+        compiler_params=pltpu.CompilerParams(vmem_limit_bytes=62 * 2**20),
+    )(*given)
 
 
 def solution(mesh):

time: 125 us -> 115 us (0.920)
  other arithmetic: 6.55 us -> 0 us
  local copies, waits for them, and re-layouts: 5.68 us -> 0 us
  Pallas kernels: 112 us -> 114 us
    convert_element_type x4 -> x0, other arithmetic: 6.55 us -> none  [the longest x1 2.84 us: shards(): up.astype(F32)]
    unnamed x36 -> x0, local copies, waits for them, and re-layouts: 5.68 us -> none
    pallas_call x0 -> x1, Pallas kernels: none -> 5.56 us  [shards(): pl.pallas_call(finish, out_shape=(wide(128, 1024, BF), wide(128, 1024, BF...]
    pallas_call x1, Pallas kernels: 112 us -> 109 us  [block_call(): pl.pallas_call(kernel, out_shape=(jax.ShapeDtypeStruct((128, 1024), BF),...]
where the time goes in v4:
time: 115 us
  Pallas kernels  114 us (99%)
    pallas_call x1, Pallas kernels, block_call(): pl.pallas_call(kernel, out_shape=(jax.ShapeDtypeStruct((128, 1024), BF),...  109 us
    pallas_call x1, Pallas kernels, shards(): pl.pallas_call(finish, out_shape=(wide(128, 1024, BF), wide(128, 1024, BF...  5.56 us

profile of v4, /device:TPU:1, one launch (start us, length us, event | category | flops | bytes accessed | tf_op | source)
XLA Modules:
  0.0 115.2 jit_solution(15044111741099234196)
XLA Ops:
  0.7 108.9 %shard_map.254 = (bf16[128,1024]{1,0:T(8,128)(2,1)}, bf16[128,1024]{1,0:T(8,128)(2,1)}, bf16[4,2,80,1024]{3,2,1,0:T(8,128)(2,1)}, bf16[2,4,512,128]{3,2,1,0:T(8,...) custom-call(bf16[128,1024]{1,0:T(8,128)(2,1)} %hid_ref.1, bf16[128,1024]{1,0:T(8,128)(2,1)} %g_ref.1, ...), custom_call_target="tpu_custom_call" | custom-call | tf_op jit(solution)/shard_map/pallas_call | solution.py:670
  109.5 5.6 %shard_map.255 = (bf16[128,1024]{1,0:T(8,128)(2,1)}, bf16[128,1024]{1,0:T(8,128)(2,1)}, f32[128]{0:T(128)}, f32[128]{0:T(128)}, f32[128]{0:T(128)}, /*index=5*/f...) custom-call(bf16[128,1024]{1,0:T(8,128)(2,1)} %get-tuple-element.20., ...), custom_call_target="tpu_custom_call" | custom-call | tf_op jit(solution)/shard_map/pallas_call | solution.py:755

commit v5 on v4

--- a/solution.py
+++ b/solution.py
@@ -450,6 +450,25 @@
     G1[512:640] = nn(CTXT[...], grads).astype(BF)
     y1 = along_y(G1, R1, 80)
 
+    CG[...] = jnp.zeros_like(CG)
+    CDG[...] = jnp.zeros_like(CDG)
+
+    @pl.loop(0, 4)
+    def _(i):
+        at = rows(256 * i, 256)
+        cols = lanes(256 * i, 256)
+        block = GB[i].reshape(256, 1024)
+        CG[...] += fold(block.astype(F32))
+        gate_grad = (nt(block, WN[...]) * GP[at]).astype(BF)
+        DG[at] = gate_grad
+        wide = gate_grad.astype(F32)
+        CDG[...] += fold(wide)
+        DGT[:, cols] = jnp.transpose(wide).astype(BF)
+
+    put(G2, nn(DGT[...], N2[...]))
+    near2 = near_start(G2, X2, 64)
+    out_z = scatter_z(out_cores, PB, PRA, PRT, PRZ)
+
     low_256 = lax.broadcasted_iota(jnp.int32, (256, 128), 1) < 64
     low_t256 = lax.broadcasted_iota(jnp.int32, (128, 256), 0) < 64
 
@@ -482,8 +501,8 @@
             DV[0:top] += nn(probs, DCM[head, q])
 
     attention_back(0)
-    out_z = scatter_z(out_cores, PB, PRA, PRT, PRZ)
     attention_back(1)
+    spread2 = spread_start(near2, G2, X2, C2, R2, 64)
 
     QKP[0:128] = DQT[...]
     QKP[128:256] = jnp.transpose(DK[...])
@@ -499,24 +518,6 @@
     near3 = near_start(G3, X3, 48)
     M[:, 0:256] = jnp.transpose(QKP[...]).astype(BF)
     M[:, 256:384] = DV[...].astype(BF)
-    CG[...] = jnp.zeros_like(CG)
-    CDG[...] = jnp.zeros_like(CDG)
-
-    @pl.loop(0, 4)
-    def _(i):
-        at = rows(256 * i, 256)
-        cols = lanes(256 * i, 256)
-        block = GB[i].reshape(256, 1024)
-        CG[...] += fold(block.astype(F32))
-        gate_grad = (nt(block, WN[...]) * GP[at]).astype(BF)
-        DG[at] = gate_grad
-        wide = gate_grad.astype(F32)
-        CDG[...] += fold(wide)
-        DGT[:, cols] = jnp.transpose(wide).astype(BF)
-
-    put(G2, nn(DGT[...], N2[...]))
-    near2 = near_start(G2, X2, 64)
-
     SUMS[...] = jnp.zeros_like(SUMS)
     in_cores = []
     in_z = []
@@ -540,13 +541,7 @@
         in_z.append(remote(DRT.at[j], DRZ.at[j], z_to(zz)))
 
     norm_grads(across_z)
-    spread3 = spread_start(near3, G3, X3, C3, R3, 48)
     norm_grads(ahead)
-    norm_send(0)
-    norm_grads(behind)
-    norm_send(1)
-    norm_grads(z)
-    norm_send(2)
     arrived(y1)
     CY1[...] = (
         G1[rows(160 * y, 160)].astype(F32) + R1[0].astype(F32) + R1[1].astype(F32) + R1[2].astype(F32)
@@ -556,7 +551,15 @@
         remote(CY1.at[rows(80 * (1 - h), 80)], X1.at[1], x_far, off, home),
         remote(CY1.at[rows(80 * (1 - h), 80)], X1.at[2], h_peer, home, home),
     ]
+    norm_send(0)
+    norm_grads(behind)
+    norm_send(1)
+    norm_grads(z)
+    norm_send(2)
+    spread3 = spread_start(near3, G3, X3, C3, R3, 48)
     out_x = scatter_x(out_z, PB, PRA, PRZ, PFX, PRX)
+    spread_sum(spread2, C2, R2, S2, 64)
+    turn2 = turn(S2, f2_ref, 64)
 
     SV[...] = jnp.zeros_like(SV)
     bias_grad = jnp.sum(fold(M[...].astype(F32)), axis=0, keepdims=True)
@@ -574,9 +577,6 @@
     SV[b, 12:13] = jnp.sum(CG[:, lanes(128 * b, 128)], axis=0, keepdims=True)
     vectors = [remote(SV.at[flip(s, m)], SVR.at[m - 1], shard_to(m)) for m in range(1, 8)]
 
-    spread2 = spread_start(near2, G2, X2, C2, R2, 64)
-    spread_sum(spread3, C3, R3, S3, 48)
-    turn3 = turn(S3, f3_ref, 48)
     arrived(x1)
 
     @pl.when(home)
@@ -589,25 +589,28 @@
     give1 = [remote(S1, f1_ref.at[y, h], chip_to(m), home, home) for m in range(1, 8)]
     scatter_end(out_x, PRX)
     out_ref[...] = (OWNH[...].astype(F32) + ACC[...] + VEC[4:5]).astype(BF)
-    give3 = give_y(turn3, f3_ref, 48)
+    spread_sum(spread3, C3, R3, S3, 48)
+    turn3 = turn(S3, f3_ref, 48)
+    give2 = give_y(turn2, f2_ref, 64)
     arrived(vectors)
     total = SV[s]
     for m in range(7):
         total = total + SVR[m]
     LV[...] = total
     pair_v = remote(LV, LVX, partner)
-    spread_sum(spread2, C2, R2, S2, 64)
-    turn2 = turn(S2, f2_ref, 64)
     in_cores[3].wait_recv()
     in_x = scatter_x(in_z, DB, DRA, DRZ, DFX, DRX)
     pair_v.wait_recv()
     LC[...] = LV[...] + LVX[...]
     LCR[chip] = LC[...]
     spread_v = [remote(LC, LCR.at[chip], chip_to(m)) for m in range(1, 8)]
-    give2 = give_y(turn2, f2_ref, 64)
-    arrived(give1)
-    last1 = [remote(f1_ref, f1_ref, partner, home, off)]
-    last3 = give_core(give3, f3_ref, 48)
+    give3 = give_y(turn3, f3_ref, 48)
+    last1 = [remote(f1_ref.at[y, h], f1_ref.at[y, h], partner, home, off)]
+    for m in range(1, 8):
+        give1[m - 1].wait_recv()
+        piece = f1_ref.at[flip(y, m % 4), flip(h, m // 4)]
+        last1.append(remote(piece, piece, partner, home, off))
+    last2 = give_core(give2, f2_ref, 64)
 
     scatter_end(in_x, DRX)
     block = OWNH[...].astype(F32)
@@ -624,7 +627,7 @@
     for m in range(1, 8):
         total = total + LCR[m]
     vec_ref[...] = total
-    last2 = give_core(give2, f2_ref, 64)
+    last3 = give_core(give3, f3_ref, 48)
     arrived(last1)
     arrived(last2)
     arrived(last3)

time: 115 us -> 114 us (level)
  Pallas kernels: 114 us -> 112 us
    pallas_call x1, Pallas kernels: 109 us -> 107 us  [block_call(): pl.pallas_call(kernel, out_shape=(jax.ShapeDtypeStruct((128, 1024), BF),...]
where the time goes in v5:
time: 114 us; the launch traced here: 113 us
  Pallas kernels  112 us (98%)
    pallas_call x1, Pallas kernels, block_call(): pl.pallas_call(kernel, out_shape=(jax.ShapeDtypeStruct((128, 1024), BF),...  107 us
    pallas_call x1, Pallas kernels, shards(): pl.pallas_call(finish, out_shape=(wide(128, 1024, BF), wide(128, 1024, BF...  5.56 us

profile of v5, /device:TPU:1, one launch (start us, length us, event | category | flops | bytes accessed | tf_op | source)
XLA Modules:
  0.0 113.3 jit_solution(9969472475160303196)
XLA Ops:
  0.7 106.9 %shard_map.254 = (bf16[128,1024]{1,0:T(8,128)(2,1)}, bf16[128,1024]{1,0:T(8,128)(2,1)}, bf16[4,2,80,1024]{3,2,1,0:T(8,128)(2,1)}, bf16[2,4,512,128]{3,2,1,0:T(8,...) custom-call(bf16[128,1024]{1,0:T(8,128)(2,1)} %hid_ref.1, bf16[128,1024]{1,0:T(8,128)(2,1)} %g_ref.1, ...), custom_call_target="tpu_custom_call" | custom-call | tf_op jit(solution)/shard_map/pallas_call | solution.py:673
  107.6 5.6 %shard_map.255 = (bf16[128,1024]{1,0:T(8,128)(2,1)}, bf16[128,1024]{1,0:T(8,128)(2,1)}, f32[128]{0:T(128)}, f32[128]{0:T(128)}, f32[128]{0:T(128)}, /*index=5*/f...) custom-call(bf16[128,1024]{1,0:T(8,128)(2,1)} %get-tuple-element.20., ...), custom_call_target="tpu_custom_call" | custom-call | tf_op jit(solution)/shard_map/pallas_call | solution.py:758

commit v6 on v5

--- a/solution.py
+++ b/solution.py
@@ -41,7 +41,7 @@
     out_ref, ing_ref, f1_ref, f2_ref, f3_ref, vec_ref, PKO, SGO, SGX, WD, WN, OWNH, OWNG,
     HB, GB, SG, PK, WQ, WU, VEC, B24, XH, N1, N2, QKP, TAB, START, QTM, QM, KT, K, V, VT,
     GP, ACT, ACTT, PT, CTXT, CTX, DCM, DCTM, DG, DGT, DQT, DK, DV, M, MT,
-    PB, PRA, PRT, PRZ, PFX, PRX, DB, DRA, DRT, DRZ, DFX, DRX, ACC,
+    PB, PRA, PRT, PRZ, PFX, PRX, DB, DRA, DRT, DRZ, DFX, DRX, ACC, ACCO,
     G1, X1, R1, S1, CY1, G2, X2, C2, R2, S2, G3, X3, C3, R3, S3,
     SUMS, CG, CDG, SV, SVR, LV, LVX, LC, LCR,
     ssem, rsem, lsem,
@@ -349,7 +349,7 @@
         copies[3].wait_recv()
         return out
 
-    def scatter_x(copies, TB, RA, RZ, FX, RX):
+    def scatter_x(copies, TB, RA, RZ, FX, RX, ACC):
         arrived(copies)
         total = TB[z, k].astype(F32) + RA[z].astype(F32)
         for j in range(3):
@@ -358,7 +358,7 @@
         FX[...] = total.astype(BF)
         return remote(FX, RX, x_cross, off, off)
 
-    def scatter_end(copy, RX):
+    def scatter_end(copy, RX, ACC):
         copy.wait_recv()
 
         @pl.when(off)
@@ -557,7 +557,6 @@
     norm_grads(z)
     norm_send(2)
     spread3 = spread_start(near3, G3, X3, C3, R3, 48)
-    out_x = scatter_x(out_z, PB, PRA, PRZ, PFX, PRX)
     spread_sum(spread2, C2, R2, S2, 64)
     turn2 = turn(S2, f2_ref, 64)
 
@@ -587,11 +586,10 @@
         f1_ref[y, h] = S1[...]
 
     give1 = [remote(S1, f1_ref.at[y, h], chip_to(m), home, home) for m in range(1, 8)]
-    scatter_end(out_x, PRX)
-    out_ref[...] = (OWNH[...].astype(F32) + ACC[...] + VEC[4:5]).astype(BF)
     spread_sum(spread3, C3, R3, S3, 48)
     turn3 = turn(S3, f3_ref, 48)
     give2 = give_y(turn2, f2_ref, 64)
+    out_x = scatter_x(out_z, PB, PRA, PRZ, PFX, PRX, ACCO)
     arrived(vectors)
     total = SV[s]
     for m in range(7):
@@ -599,7 +597,7 @@
     LV[...] = total
     pair_v = remote(LV, LVX, partner)
     in_cores[3].wait_recv()
-    in_x = scatter_x(in_z, DB, DRA, DRZ, DFX, DRX)
+    in_x = scatter_x(in_z, DB, DRA, DRZ, DFX, DRX, ACC)
     pair_v.wait_recv()
     LC[...] = LV[...] + LVX[...]
     LCR[chip] = LC[...]
@@ -612,7 +610,9 @@
         last1.append(remote(piece, piece, partner, home, off))
     last2 = give_core(give2, f2_ref, 64)
 
-    scatter_end(in_x, DRX)
+    scatter_end(out_x, PRX, ACCO)
+    out_ref[...] = (OWNH[...].astype(F32) + ACCO[...] + VEC[4:5]).astype(BF)
+    scatter_end(in_x, DRX, ACC)
     block = OWNH[...].astype(F32)
     center = block - jnp.mean(block, axis=-1, keepdims=True)
     spread = jnp.mean(center * center, axis=-1, keepdims=True)
@@ -657,7 +657,7 @@
             vm((4, 2, 128, 1024), BF), vm((4, 128, 1024), BF), vm((3, 128, 1024), BF), vm((3, 128, 1024), BF),
             vm((128, 1024), BF), vm((128, 1024), BF),
         ]
-    scratch += [vm((128, 1024), F32)]
+    scratch += [vm((128, 1024), F32), vm((128, 1024), F32)]
     scratch += [
         vm((640, 1024), BF), vm((3, 80, 1024), BF), vm((3, 160, 1024), BF), vm((80, 1024), BF), vm((160, 1024), BF),
     ]

time: 114 us -> 118 us (1.035); the launches traced: 113 us -> 116 us
  Pallas kernels: 112 us -> 115 us
    pallas_call x1, Pallas kernels: 107 us -> 109 us  [block_call(): pl.pallas_call(kernel, out_shape=(jax.ShapeDtypeStruct((128, 1024), BF),...]
where the time goes in v6:
time: 118 us; the launch traced here: 116 us
  Pallas kernels  115 us (97%)
    pallas_call x1, Pallas kernels, block_call(): pl.pallas_call(kernel, out_shape=(jax.ShapeDtypeStruct((128, 1024), BF),...  109 us
    pallas_call x1, Pallas kernels, shards(): pl.pallas_call(finish, out_shape=(wide(128, 1024, BF), wide(128, 1024, BF...  5.56 us

profile of v6, /device:TPU:1, one launch (start us, length us, event | category | flops | bytes accessed | tf_op | source)
XLA Modules:
  0.0 115.6 jit_solution(2229702206207263803)
XLA Ops:
  0.7 109.2 %shard_map.254 = (bf16[128,1024]{1,0:T(8,128)(2,1)}, bf16[128,1024]{1,0:T(8,128)(2,1)}, bf16[4,2,80,1024]{3,2,1,0:T(8,128)(2,1)}, bf16[2,4,512,128]{3,2,1,0:T(8,...) custom-call(bf16[128,1024]{1,0:T(8,128)(2,1)} %hid_ref.1, bf16[128,1024]{1,0:T(8,128)(2,1)} %g_ref.1, ...), custom_call_target="tpu_custom_call" | custom-call | tf_op jit(solution)/shard_map/pallas_call | solution.py:673
  109.9 5.6 %shard_map.255 = (bf16[128,1024]{1,0:T(8,128)(2,1)}, bf16[128,1024]{1,0:T(8,128)(2,1)}, f32[128]{0:T(128)}, f32[128]{0:T(128)}, f32[128]{0:T(128)}, /*index=5*/f...) custom-call(bf16[128,1024]{1,0:T(8,128)(2,1)} %get-tuple-element.20., ...), custom_call_target="tpu_custom_call" | custom-call | tf_op jit(solution)/shard_map/pallas_call | solution.py:758
